TPU v7x, 128 devices: a whole 4x4x4 slice. The times are simulated.
128 devices in a mesh: src: 64 (over y, z_hi, x, core), hi: 2 (over z_lo).
Axes of the slice: x: 4, y: 4, z: 4 (z_hi: 2, z_lo: 2; z = z_hi * 2 + z_lo), core: 2. Of those that a mesh axis runs over, the one named last changes fastest.
Arguments:
- traces: bfloat16 [64, 64, 2, 64, 128], P(None, None, 'hi', 'src'), may hold values from -6 to 6
- observed: bfloat16 [64, 2, 64, 64, 128], P(None, 'hi', 'src'), may hold values from -6 to 6
- leaf_maps: bfloat16 [64, 2, 64, 64, 128], P(None, 'hi', 'src'), may hold values from -0.5 to 0.5
- level_maps: bfloat16 [13, 64, 2, 64, 64, 128], P(None, None, 'hi', 'src'), may hold values from -0.5 to 0.5
- final_maps: bfloat16 [2, 64, 64, 64, 128], P('hi', 'src'), may hold values from -0.75 to 0.75
Outputs:
- residual: bfloat16 [64, 2, 64, 64, 128], P(None, 'hi', 'src')
- gradient: bfloat16 [64, 64, 2, 64, 128], P(None, None, 'hi', 'src')
All inputs are finite; a program needn't handle non-finite values.
Results may differ from a plain program's by a relative error of at most 0.035.
Values may be sent and summed in bfloat16 or wider, within the bound.
No kernel may reach another device: no remote copies, remote signals or barrier semaphores. Data moves between devices by JAX's collectives and lax.ppermute only.
A program may use at most 128 MiB of HBM per device.

v0:
```python
import functools

import jax
import jax.numpy as jnp
from jax import lax
from jax.experimental import pallas as pl
from jax.experimental.pallas import tpu as pltpu
from jax.sharding import PartitionSpec as P

CHUNKS = 2
LANES = 128
BF = jnp.bfloat16
F32 = jnp.float32


def reverse_bits(value, bits):
    return int(format(value, f"0{bits}b")[::-1], 2)


def lane_block(shape, width):
    return lax.broadcasted_iota(jnp.int32, shape, len(shape) - 1) // width


def pick_lanes(product, rows, count, width):
    block = lane_block((rows, LANES), width)
    out = product[:rows]
    for b in range(1, count):
        out = jnp.where(block == b, product[b * rows:(b + 1) * rows], out)
    return out


def split_rows(pair):
    left = lane_block(pair.shape, LANES // 2) == 0
    zero = jnp.zeros(pair.shape, pair.dtype)
    return jnp.concatenate([jnp.where(left, pair, zero), jnp.where(left, zero, pair)], axis=0)


def halves_of(product, rows):
    first, second = product[:rows], product[rows:]
    left = lane_block((rows, LANES), LANES // 2) == 0
    low = jnp.where(left, first, pltpu.roll(second, LANES // 2, 1))
    high = jnp.where(left, pltpu.roll(first, LANES // 2, 1), second)
    return low, high


def is_high(level, src_bits):
    if level < src_bits:
        return (lax.axis_index("src") >> level & 1) == 1
    return (lax.axis_index("hi") >> (level - src_bits) & 1) == 1


def dot(a, b):
    return jnp.dot(a, b, preferred_element_type=F32)


def dot_nt(a, b):
    return lax.dot_general(a, b, (((1,), (1,)), ((), ())), preferred_element_type=F32)


def leaf_kernel(chunk, traces, leaf, token, out, held, mats, sems, wide):
    vectors, boxes, points = held.shape
    lane_boxes = LANES // vectors
    rank = mats.shape[1]
    copies = [
        pltpu.make_async_copy(traces.at[pl.ds(chunk * vectors, vectors)], held, sems.at[0]),
        pltpu.make_async_copy(leaf, mats, sems.at[1]),
    ]
    for copy in copies:
        copy.start()
    copies[0].wait()
    wide[...] = held[...].astype(F32).reshape(wide.shape)
    copies[1].wait()
    for g in range(boxes // lane_boxes):
        rows = [
            wide[pl.ds(g * lane_boxes + b, vectors, stride=boxes), :] for b in range(lane_boxes)
        ]
        stacked = jnp.concatenate(rows, axis=0).astype(BF)
        group = mats[pl.ds(g * lane_boxes, lane_boxes)].reshape(lane_boxes * rank, points)
        out[g] = pick_lanes(dot_nt(group, stacked), rank, lane_boxes, vectors).astype(BF)


def forward_group(weights, stacked, lane_boxes, rank):
    mats = weights.reshape(lane_boxes * rank, LANES)
    return pick_lanes(dot(mats, stacked), rank, lane_boxes, LANES // lane_boxes).astype(BF)


def cross_step(own, other, mats, out, high, lane_boxes):
    groups, rank = own.shape[0], own.shape[1]
    for g in range(groups):
        mine, theirs = own[g], other[g]
        take = jnp.broadcast_to(high, mine.shape)
        lower = jnp.where(take, theirs, mine)
        upper = jnp.where(take, mine, theirs)
        stacked = jnp.concatenate([lower, upper], axis=0)
        weights = mats[pl.ds(g * lane_boxes, lane_boxes)]
        out[g] = forward_group(weights, stacked, lane_boxes, rank)


def cross_kernel(level, src_bits, lane_boxes, own, other, maps, token, out):
    cross_step(own, other, maps.at[level], out, is_high(level, src_bits), lane_boxes)


def local_forward(lane_boxes, maps, first, out, work):
    groups, rank = out.shape[0], out.shape[1]
    lane_bits = lane_boxes.bit_length() - 1
    box_bits = maps.shape[1].bit_length() - 1
    for bit in range(box_bits):
        mats = maps.at[first + bit]
        source = work.at[bit % 2]
        target = out if bit == box_bits - 1 else work.at[(bit + 1) % 2]
        if bit < lane_bits:
            shift = LANES // lane_boxes << bit
            for g in range(groups):
                value = source[g].astype(F32)
                is_set = (lane_block(value.shape, shift) & 1) == 1
                lower = jnp.where(is_set, pltpu.roll(value, shift, 1), value)
                upper = jnp.where(is_set, value, pltpu.roll(value, LANES - shift, 1))
                stacked = jnp.concatenate([lower, upper], axis=0).astype(BF)
                weights = mats[pl.ds(g * lane_boxes, lane_boxes)]
                target[g] = forward_group(weights, stacked, lane_boxes, rank)
        else:
            inner = 1 << bit - lane_bits
            for g0 in range(groups):
                if g0 & inner:
                    continue
                stacked = jnp.concatenate([source[g0], source[g0 + inner]], axis=0)
                for g in (g0, g0 + inner):
                    weights = mats[pl.ds(g * lane_boxes, lane_boxes)]
                    target[g] = forward_group(weights, stacked, lane_boxes, rank)


def prepare_kernel(final_maps, observed, token, out, final, held, sems, wide):
    vectors, boxes, points = held.shape
    rank = final.shape[1]
    box_bits = boxes.bit_length() - 1
    fetch_maps = pltpu.make_async_copy(final_maps, final, sems.at[1])
    fetch_maps.start()
    fetch = pltpu.make_async_copy(observed, held, sems.at[0])
    fetch.start()
    fetch_maps.wait()
    for p in range(boxes // 2):
        mats = pair_final(final, p, box_bits)
        out[0, p] = pick_lanes(dot_nt(mats, mats), rank, 2, rank).astype(BF)
    fetch.wait()
    wide[...] = held[...].astype(F32).reshape(wide.shape)
    for p in range(boxes // 2):
        rows = [
            wide[pl.ds(reverse_bits(k, box_bits), vectors, stride=boxes), :]
            for k in (2 * p, 2 * p + 1)
        ]
        product = dot_nt(jnp.concatenate(rows, axis=0).astype(BF), pair_final(final, p, box_bits))
        out[1, p] = pick_lanes(product, vectors, 2, rank).astype(BF)


def pair_final(final, p, box_bits):
    return jnp.concatenate(
        [final[reverse_bits(2 * p, box_bits)], final[reverse_bits(2 * p + 1, box_bits)]], axis=0
    )


def residual_kernel(chunk, coeffs, final_maps, observed, *refs):
    residual, done, final, held, sems, wide, result = refs[-7:]
    groups = coeffs.shape[0]
    vectors, boxes, points = held.shape
    box_bits = boxes.bit_length() - 1
    lane_boxes = LANES // vectors
    own_rows = pl.ds(chunk * vectors, vectors)
    fetch_maps = pltpu.make_async_copy(final_maps, final, sems.at[1])
    fetch_maps.start()
    fetch = pltpu.make_async_copy(observed.at[own_rows], held, sems.at[0])
    fetch.start()
    fetch.wait()
    wide[...] = held[...].astype(F32).reshape(wide.shape)
    fetch_maps.wait()
    done[...] = jnp.zeros(done.shape, done.dtype)
    for g in range(groups):
        turned = jnp.transpose(coeffs[g].astype(F32)).astype(BF)
        for b in range(lane_boxes):
            t = reverse_bits(g * lane_boxes + b, box_bits)
            value = dot(turned[b * vectors:(b + 1) * vectors], final[t])
            rows = pl.ds(t, vectors, stride=boxes)
            result[rows, :] = value - wide[rows, :]
    held[...] = result[...].reshape(held.shape).astype(BF)
    store = pltpu.make_async_copy(held, residual.at[own_rows], sems.at[1])
    store.start()
    store.wait()


def adjoint_cross_pair(value, mats, kept, sent, p, high):
    rows = value.shape[0]
    low, upper = halves_of(dot(split_rows(value), mats), rows)
    take = jnp.broadcast_to(high, low.shape)
    kept[p] = jnp.where(take, upper, low)
    sent[p] = jnp.where(take, low, upper).astype(BF)


def pair_rows(mats, p):
    rank = mats.shape[1]
    return mats[pl.ds(2 * p, 2)].reshape(2 * rank, LANES)


def local_adjoint(maps, first, work):
    pairs, vectors = work.shape[1], work.shape[2]
    box_bits = maps.shape[1].bit_length() - 1
    for step, bit in enumerate(reversed(range(box_bits))):
        mats = maps.at[first + bit]
        source = work.at[step % 2]
        target = work.at[(step + 1) % 2]
        if bit == 0:
            for p in range(pairs):
                target[p] = dot(source[p], pair_rows(mats, p)).astype(BF)
        else:
            inner = 1 << bit - 1
            for p0 in range(pairs):
                if p0 & inner:
                    continue
                p1 = p0 + inner
                rows = jnp.concatenate([split_rows(source[p0]), split_rows(source[p1])], axis=1)
                stacked = jnp.concatenate([pair_rows(mats, p0), pair_rows(mats, p1)], axis=0)
                low, upper = halves_of(dot(rows, stacked), vectors)
                target[p0] = low.astype(BF)
                target[p1] = upper.astype(BF)
    return work.at[box_bits % 2]


def middle_kernel(
    level, src_bits, lane_boxes, chunk, own, other, maps, normal, token,
    coeffs, kept, sent, work, pair_work,
):
    groups, rank = own.shape[0], own.shape[1]
    pairs, vectors = kept.shape[0], kept.shape[1]
    high = is_high(level, src_bits)
    cross_step(own, other, maps.at[level], work.at[0], high, lane_boxes)
    local_forward(lane_boxes, maps, level + 1, coeffs, work)
    for g in range(groups):
        turned = jnp.transpose(coeffs[g].astype(F32)).astype(BF)
        for i in range(lane_boxes // 2):
            p = g * lane_boxes // 2 + i
            product = dot(turned[2 * i * vectors:2 * (i + 1) * vectors], normal[0, p])
            value = pick_lanes(product, vectors, 2, rank)
            wanted = normal[1, p, pl.ds(chunk * vectors, vectors), :].astype(F32)
            pair_work[0, p] = (value - wanted).astype(BF)
    source = local_adjoint(maps, level + 1, pair_work)
    for p in range(pairs):
        adjoint_cross_pair(source[p], pair_rows(maps.at[level], p), kept, sent, p, high)


def adjoint_cross_kernel(level, src_bits, held_part, received, maps, token, kept, sent):
    high = is_high(level, src_bits)
    for p in range(held_part.shape[0]):
        value = (held_part[p] + received[p].astype(F32)).astype(BF)
        adjoint_cross_pair(value, pair_rows(maps.at[level], p), kept, sent, p, high)


def gradient_kernel(chunk, held_part, received, leaf, *refs):
    gradient, held, sems, result = refs[-4:]
    pairs, vectors = held_part.shape[0], held_part.shape[1]
    boxes = leaf.shape[0]
    for p in range(pairs):
        value = (held_part[p] + received[p].astype(F32)).astype(BF)
        product = dot(split_rows(value), pair_rows(leaf, p))
        result[pl.ds(2 * p, vectors, stride=boxes), :] = product[:vectors]
        result[pl.ds(2 * p + 1, vectors, stride=boxes), :] = product[vectors:]
    held[...] = result[...].reshape(held.shape).astype(BF)
    store = pltpu.make_async_copy(
        held, gradient.at[pl.ds(chunk * vectors, vectors)], sems.at[0]
    )
    store.start()
    store.wait()


VMEM = pl.BlockSpec(memory_space=pltpu.VMEM)
ANY = pl.BlockSpec(memory_space=pl.ANY)
HBM = pl.BlockSpec(memory_space=pltpu.HBM)


def call(kernel, out_shape, in_specs, out_specs, scratch, flops, moved, limit, aliases=None):
    return pl.pallas_call(
        kernel,
        out_shape=out_shape,
        in_specs=in_specs,
        out_specs=out_specs,
        scratch_shapes=scratch,
        input_output_aliases=aliases or {},
        compiler_params=pltpu.CompilerParams(vmem_limit_bytes=limit << 20),
        cost_estimate=pl.CostEstimate(flops=flops, bytes_accessed=moved, transcendentals=0),
    )


def body(traces, observed, leaf_maps, level_maps, final_maps):
    total = traces.shape[0]
    boxes, points = traces.shape[1], traces.shape[4]
    rank = leaf_maps.shape[3]
    src_count, hi_count = lax.axis_size("src"), lax.axis_size("hi")
    src_bits = src_count.bit_length() - 1
    hi_bits = hi_count.bit_length() - 1
    device_bits = src_bits + hi_bits
    box_bits = boxes.bit_length() - 1
    vectors = total // CHUNKS
    lane_boxes = LANES // vectors
    groups, pairs = boxes // lane_boxes, boxes // 2

    leaf = leaf_maps.reshape(boxes, rank, points)
    final = final_maps.reshape(boxes, rank, points)
    levels = level_maps.reshape(level_maps.shape[0], boxes, rank, 2 * rank)
    samples = traces.reshape(total, boxes, points)
    wanted = observed.reshape(total, boxes, points)

    def shape(*dims, dtype=BF):
        return jax.ShapeDtypeStruct(dims, dtype)

    forward_shape = shape(groups, rank, LANES)
    pair_shape = shape(pairs, vectors, LANES)
    kept_shape = shape(pairs, vectors, LANES, dtype=F32)
    sample_shape = shape(vectors, boxes, points)
    full_shape = shape(total, boxes, points)
    wide = pltpu.VMEM((vectors * boxes, points), F32)
    held = pltpu.VMEM((vectors, boxes, points), BF)
    sems = pltpu.SemaphoreType.DMA((2,))
    flops = 2 * boxes * rank * 2 * rank * vectors
    moved = boxes * rank * 2 * rank * 2

    def exchange(array, level):
        if level < src_bits:
            axis, count, bit = "src", src_count, level
        else:
            axis, count, bit = "hi", hi_count, level - src_bits
        return lax.ppermute(array, axis, [(i, i ^ 1 << bit) for i in range(count)])

    def reversal(array):
        pairs_of = []
        for src in range(src_count):
            for hi in range(hi_count):
                there = reverse_bits(hi * src_count + src, device_bits)
                pairs_of.append(
                    (src * hi_count + hi, there % src_count * hi_count + there // src_count)
                )
        return lax.ppermute(array, ("src", "hi"), pairs_of)

    def leaf_call(chunk):
        kernel = functools.partial(leaf_kernel, chunk)
        scratch = [held, pltpu.VMEM((boxes, rank, points), BF), sems, wide]
        return call(kernel, forward_shape, [HBM, HBM, ANY], VMEM, scratch, flops, 2 * moved, 8)

    def prepare(*operands):
        scratch = [
            pltpu.VMEM((boxes, rank, points), BF), pltpu.VMEM((total, boxes, points), BF), sems,
            pltpu.VMEM((total * boxes, points), F32),
        ]
        return call(
            prepare_kernel, shape(2, pairs, total, LANES), [HBM, HBM, ANY], VMEM, scratch,
            4 * flops, 4 * moved, 8,
        )(*operands)

    def residual_call(chunk, *operands):
        kernel = functools.partial(residual_kernel, chunk)
        specs = [VMEM, HBM, HBM, ANY] + [HBM] * (len(operands) - 4)
        scratch = [pltpu.VMEM((boxes, rank, points), BF), held, sems, wide, wide]
        return call(
            kernel, (full_shape, shape(8, LANES, dtype=F32)), specs, (HBM, VMEM), scratch,
            flops, 2 * moved, 8, {4: 0} if len(operands) > 4 else None,
        )(*operands)

    def gradient_call(chunk, *operands):
        kernel = functools.partial(gradient_kernel, chunk)
        specs = [VMEM] * 3 + [HBM] * (len(operands) - 3)
        return call(
            kernel, full_shape, specs, HBM, [held, sems, wide],
            flops, 2 * moved, 8, {3: 0} if len(operands) > 3 else None,
        )(*operands)

    def cross_call(level):
        kernel = functools.partial(cross_kernel, level, src_bits, lane_boxes)
        return call(kernel, forward_shape, [VMEM] * 3 + [ANY], VMEM, [], flops, moved, 4)

    def adjoint_call(level):
        kernel = functools.partial(adjoint_cross_kernel, level, src_bits)
        return call(
            kernel, (kept_shape, pair_shape), [VMEM] * 3 + [ANY], (VMEM, VMEM), [], flops, moved, 4
        )

    def middle_call(chunk):
        kernel = functools.partial(middle_kernel, top, src_bits, lane_boxes, chunk)
        scratch = [
            pltpu.VMEM((2, groups, rank, LANES), BF),
            pltpu.VMEM((2, pairs, vectors, LANES), BF),
        ]
        return call(
            kernel, (forward_shape, kept_shape, pair_shape), [VMEM] * 4 + [ANY], (VMEM,) * 3,
            scratch, 15 * flops, 15 * moved, 8,
        )

    top = device_bits - 1
    token = leaf
    coeffs, kept, sent, target = [None] * CHUNKS, [None] * CHUNKS, [None] * CHUNKS, [None] * CHUNKS
    every = range(CHUNKS)
    for c in every:
        coeffs[c] = token = leaf_call(c)(samples, leaf, token)
    normal = None
    for level in range(top):
        for c in every:
            maps = levels if level else levels[:1]
            token = cross_call(level)(coeffs[c], exchange(coeffs[c], level), maps, token)
            coeffs[c] = token
        if level == 0:
            normal = token = prepare(final, wanted, token)
            normal = reversal(normal)
    for c in every:
        target[c], kept[c], sent[c] = middle_call(c)(
            coeffs[c], exchange(coeffs[c], top), levels, normal, token
        )
        token = sent[c]
    residual, gradient = (), ()
    for level in reversed(range(top)):
        for c in every:
            kept[c], sent[c] = adjoint_call(level)(
                kept[c], exchange(sent[c], level + 1), levels, token
            )
            token = sent[c]
        if level == 1:
            for c in every:
                operands = (reversal(target[c]), final, wanted, token, *residual)
                *residual, token = residual_call(c, *operands)
    for c in every:
        gradient = [gradient_call(c, kept[c], exchange(sent[c], 0), leaf, *gradient)]
    residual, gradient = residual[0], gradient[0]
    return (
        residual.reshape(total, 1, 1, boxes, points),
        gradient.reshape(total, boxes, 1, 1, points),
    )


def solution(mesh):
    placed = (
        P(None, None, "hi", "src", None),
        P(None, "hi", "src", None, None),
        P(None, "hi", "src", None, None),
        P(None, None, "hi", "src", None, None),
        P("hi", "src", None, None, None),
    )
    return jax.shard_map(
        body,
        mesh=mesh,
        in_specs=placed,
        out_specs=(P(None, "hi", "src", None, None), P(None, None, "hi", "src", None)),
        check_vma=False,
    )
```

profile of v0, /device:TPU:1, one launch (start us, length us, event | category | flops | bytes accessed | tf_op | source)
XLA Modules:
  0.0 208.1 jit_solution(5848285969832707100)
XLA Ops:
  13.4 2.4 %shard_map.72.token = bf16[2,32,64,128]{3,2,1,0:T(8,128)(2,1)S(1)} custom-call(bf16[64,64,128]{2,1,0:T(8,128)(2,1)S(1)} %bitcast.44, bf16[64,64,128]{2,1,0:T(8,128)(2,1)S(1)} %bitcast.47, bf16[16,64,128]{2,1,0:T(8,128)(2,1)S(1)} %shard_map.71.token.own), custom_call_target="tpu_custom_call" | custom-call | flops 134217728 | bytes 4194304 | tf_op jit(solution)/shard_map/pallas_call | solution.py:350
  16.8 2.9 %collective-permute-start.5 = (bf16[16,64,128]{2,1,0:T(8,128)(2,1)S(1)}, bf16[16,64,128]{2,1,0:T(8,128)(2,1)S(1)}, u32[]{:S(2)}, u32[]{:S(2)}) collective-permute-start(bf16[16,64,128]{2,1,0:T(8,128)(2,1)S(1)} %shard_map.73.token.own), channel_id=1, source_target_pairs={{0,8},{2,10},{4,12},{6,14},{8,0},{10,2},{12,4},{14,6},{16,24},{18,... | collective-permute-start | bytes 786440 | tf_op jit(solution)/shard_map/ppermute | solution.py:328
  19.7 2.3 %collective-permute-done.2.other = bf16[16,64,128]{2,1,0:T(8,128)(2,1)S(1)} collective-permute-done((bf16[16,64,128]{2,1,0:T(8,128)(2,1)S(1)}, bf16[16,64,128]{2,1,0:T(8,128)(2,1)S(1)}, u32[]{:S(2)}, u32[]{:S(2)}) %collective-permute-start.2) | collective-permute-done | bytes 262176 | tf_op jit(solution)/shard_map/ppermute | solution.py:328
  22.4 2.9 %collective-permute-start.4 = (bf16[16,64,128]{2,1,0:T(8,128)(2,1)S(1)}, bf16[16,64,128]{2,1,0:T(8,128)(2,1)S(1)}, u32[]{:S(2)}, u32[]{:S(2)}) collective-permute-start(bf16[16,64,128]{2,1,0:T(8,128)(2,1)S(1)} %shard_map.74.token.own), channel_id=1, source_target_pairs={{0,8},{2,10},{4,12},{6,14},{8,0},{10,2},{12,4},{14,6},{16,24},{18,... | collective-permute-start | bytes 786440 | tf_op jit(solution)/shard_map/ppermute | solution.py:328
  25.3 4.5 %collective-permute-done.5.other = bf16[16,64,128]{2,1,0:T(8,128)(2,1)S(1)} collective-permute-done((bf16[16,64,128]{2,1,0:T(8,128)(2,1)S(1)}, bf16[16,64,128]{2,1,0:T(8,128)(2,1)S(1)}, u32[]{:S(2)}, u32[]{:S(2)}) %collective-permute-start.5) | collective-permute-done | bytes 262176 | tf_op jit(solution)/shard_map/ppermute | solution.py:328
  30.3 3.7 %collective-permute-start.7 = (bf16[16,64,128]{2,1,0:T(8,128)(2,1)S(1)}, bf16[16,64,128]{2,1,0:T(8,128)(2,1)S(1)}, u32[]{:S(2)}, u32[]{:S(2)}) collective-permute-start(bf16[16,64,128]{2,1,0:T(8,128)(2,1)S(1)} %shard_map.75.token.own), channel_id=1, source_target_pairs={{0,16},{2,18},{4,20},{6,22},{8,24},{10,26},{12,28},{14,30},{16,0},... | collective-permute-start | bytes 786440 | tf_op jit(solution)/shard_map/ppermute | solution.py:328
  34.0 5.1 %collective-permute-start.13 = (bf16[2,32,64,128]{3,2,1,0:T(8,128)(2,1)S(1)}, bf16[2,32,64,128]{3,2,1,0:T(8,128)(2,1)S(1)}, u32[]{:S(2)}, u32[]{:S(2)}) collective-permute-start(bf16[2,32,64,128]{3,2,1,0:T(8,128)(2,1)S(1)} %shard_map.72.token), channel_id=1, source_target_pairs={{0,0},{1,2},{2,1},{3,3},{4,64},{5,66},{6,65},{7,67},{8,32},{9,34},... | collective-permute-start | bytes 3145736 | tf_op jit(solution)/shard_map/ppermute | solution.py:338
  40.9 1.5 collective-permute-start.9
  42.4 15.3 %collective-permute-done.6.other = bf16[16,64,128]{2,1,0:T(8,128)(2,1)S(1)} collective-permute-done((bf16[16,64,128]{2,1,0:T(8,128)(2,1)S(1)}, bf16[16,64,128]{2,1,0:T(8,128)(2,1)S(1)}, u32[]{:S(2)}, u32[]{:S(2)}) %collective-permute-start.6) | collective-permute-done | bytes 262176 | tf_op jit(solution)/shard_map/ppermute | solution.py:328
  58.2 35.1 %collective-permute-done.9.other = bf16[16,64,128]{2,1,0:T(8,128)(2,1)S(1)} collective-permute-done((bf16[16,64,128]{2,1,0:T(8,128)(2,1)S(1)}, bf16[16,64,128]{2,1,0:T(8,128)(2,1)S(1)}, u32[]{:S(2)}, u32[]{:S(2)}) %collective-permute-start.9) | collective-permute-done | bytes 262176 | tf_op jit(solution)/shard_map/ppermute | solution.py:328
  93.8 5.1 %collective-permute-done.8.other = bf16[16,64,128]{2,1,0:T(8,128)(2,1)S(1)} collective-permute-done((bf16[16,64,128]{2,1,0:T(8,128)(2,1)S(1)}, bf16[16,64,128]{2,1,0:T(8,128)(2,1)S(1)}, u32[]{:S(2)}, u32[]{:S(2)}) %collective-permute-start.8) | collective-permute-done | bytes 262176 | tf_op jit(solution)/shard_map/ppermute | solution.py:328
  99.4 5.1 %collective-permute-done.11.other = bf16[16,64,128]{2,1,0:T(8,128)(2,1)S(1)} collective-permute-done((bf16[16,64,128]{2,1,0:T(8,128)(2,1)S(1)}, bf16[16,64,128]{2,1,0:T(8,128)(2,1)S(1)}, u32[]{:S(2)}, u32[]{:S(2)}) %collective-permute-start.11) | collective-permute-done | bytes 262176 | tf_op jit(solution)/shard_map/ppermute | solution.py:328
  105.1 5.1 %collective-permute-done.10.other = bf16[16,64,128]{2,1,0:T(8,128)(2,1)S(1)} collective-permute-done((bf16[16,64,128]{2,1,0:T(8,128)(2,1)S(1)}, bf16[16,64,128]{2,1,0:T(8,128)(2,1)S(1)}, u32[]{:S(2)}, u32[]{:S(2)}) %collective-permute-start.10) | collective-permute-done | bytes 262176 | tf_op jit(solution)/shard_map/ppermute | solution.py:328
  112.2 4.4 %shard_map.83 = (bf16[16,64,128]{2,1,0:T(8,128)(2,1)S(1)}, f32[32,32,128]{2,1,0:T(8,128)S(1)}, bf16[32,32,128]{2,1,0:T(8,128)(2,1)S(1)}) custom-call(bf16[16,64,128]{2,1,0:T(8,128)(2,1)S(1)} %shard_map.81.token.own, bf16[16,64,128]{2,1,0:T(8,128)(2,1)S(1)} %collective-permute-done.14.other, bf16[13,64,64,128]{3,2,1,0:T(8,128)(2,1)S(1)} %bitcast.25, ...), custom_call_target="tpu_custom_call" | custom-call | flops 503316480 | bytes 15728640 | tf_op jit(solution)/shard_map/pallas_call | solution.py:409
  118.2 4.4 %shard_map.84 = (bf16[16,64,128]{2,1,0:T(8,128)(2,1)S(1)}, f32[32,32,128]{2,1,0:T(8,128)S(1)}, bf16[32,32,128]{2,1,0:T(8,128)(2,1)S(1)}) custom-call(bf16[16,64,128]{2,1,0:T(8,128)(2,1)S(1)} %shard_map.82.token.own, bf16[16,64,128]{2,1,0:T(8,128)(2,1)S(1)} %collective-permute-done.12.other, bf16[13,64,64,128]{3,2,1,0:T(8,128)(2,1)S(1)} %bitcast.26, ...), custom_call_target="tpu_custom_call" | custom-call | flops 503316480 | bytes 15728640 | tf_op jit(solution)/shard_map/pallas_call | solution.py:409
  123.5 3.8 %collective-permute-start.20 = (bf16[32,32,128]{2,1,0:T(8,128)(2,1)S(1)}, bf16[32,32,128]{2,1,0:T(8,128)(2,1)S(1)}, u32[]{:S(2)}, u32[]{:S(2)}) collective-permute-start(bf16[32,32,128]{2,1,0:T(8,128)(2,1)S(1)} %get-tuple-element.42.token), channel_id=1, source_target_pairs={{0,64},{2,66},{4,68},{6,70},{8,72},{10,74},{12,76},{14,78},{16,80}... | collective-permute-start | bytes 786440 | tf_op jit(solution)/shard_map/ppermute | solution.py:328
  127.3 1.8 collective-permute-done.17.received
  129.6 3.8 %collective-permute-start.19 = (bf16[32,32,128]{2,1,0:T(8,128)(2,1)S(1)}, bf16[32,32,128]{2,1,0:T(8,128)(2,1)S(1)}, u32[]{:S(2)}, u32[]{:S(2)}) collective-permute-start(bf16[32,32,128]{2,1,0:T(8,128)(2,1)S(1)} %get-tuple-element.44.token), channel_id=1, source_target_pairs={{0,64},{2,66},{4,68},{6,70},{8,72},{10,74},{12,76},{14,78},{16,80}... | collective-permute-start | bytes 786440 | tf_op jit(solution)/shard_map/ppermute | solution.py:328
  133.9 3.7 %collective-permute-done.19.received = bf16[32,32,128]{2,1,0:T(8,128)(2,1)S(1)} collective-permute-done((bf16[32,32,128]{2,1,0:T(8,128)(2,1)S(1)}, bf16[32,32,128]{2,1,0:T(8,128)(2,1)S(1)}, u32[]{:S(2)}, u32[]{:S(2)}) %collective-permute-start.19) | collective-permute-done | bytes 262176 | tf_op jit(solution)/shard_map/ppermute | solution.py:328
  138.4 3.8 %collective-permute-done.22.received = bf16[32,32,128]{2,1,0:T(8,128)(2,1)S(1)} collective-permute-done((bf16[32,32,128]{2,1,0:T(8,128)(2,1)S(1)}, bf16[32,32,128]{2,1,0:T(8,128)(2,1)S(1)}, u32[]{:S(2)}, u32[]{:S(2)}) %collective-permute-start.22) | collective-permute-done | bytes 262176 | tf_op jit(solution)/shard_map/ppermute | solution.py:328
  142.9 4.9 %collective-permute-done.21.received = bf16[32,32,128]{2,1,0:T(8,128)(2,1)S(1)} collective-permute-done((bf16[32,32,128]{2,1,0:T(8,128)(2,1)S(1)}, bf16[32,32,128]{2,1,0:T(8,128)(2,1)S(1)}, u32[]{:S(2)}, u32[]{:S(2)}) %collective-permute-start.21) | collective-permute-done | bytes 262176 | tf_op jit(solution)/shard_map/ppermute | solution.py:328
  150.0 2.5 %collective-permute-start.26 = (bf16[32,32,128]{2,1,0:T(8,128)(2,1)S(1)}, bf16[32,32,128]{2,1,0:T(8,128)(2,1)S(1)}, u32[]{:S(2)}, u32[]{:S(2)}) collective-permute-start(bf16[32,32,128]{2,1,0:T(8,128)(2,1)S(1)} %get-tuple-element.54.token), channel_id=1, source_target_pairs={{0,8},{2,10},{4,12},{6,14},{8,0},{10,2},{12,4},{14,6},{16,24},{18,... | collective-permute-start | bytes 786440 | tf_op jit(solution)/shard_map/ppermute | solution.py:328
  152.5 4.8 %collective-permute-done.23.received = bf16[32,32,128]{2,1,0:T(8,128)(2,1)S(1)} collective-permute-done((bf16[32,32,128]{2,1,0:T(8,128)(2,1)S(1)}, bf16[32,32,128]{2,1,0:T(8,128)(2,1)S(1)}, u32[]{:S(2)}, u32[]{:S(2)}) %collective-permute-start.23) | collective-permute-done | bytes 262176 | tf_op jit(solution)/shard_map/ppermute | solution.py:328
  157.8 3.1 %collective-permute-start.25 = (bf16[32,32,128]{2,1,0:T(8,128)(2,1)S(1)}, bf16[32,32,128]{2,1,0:T(8,128)(2,1)S(1)}, u32[]{:S(2)}, u32[]{:S(2)}) collective-permute-start(bf16[32,32,128]{2,1,0:T(8,128)(2,1)S(1)} %get-tuple-element.56.token), channel_id=1, source_target_pairs={{0,8},{2,10},{4,12},{6,14},{8,0},{10,2},{12,4},{14,6},{16,24},{18,... | collective-permute-start | bytes 786440 | tf_op jit(solution)/shard_map/ppermute | solution.py:328
  160.9 6.4 %collective-permute-start.16 = (bf16[16,64,128]{2,1,0:T(8,128)(2,1)S(1)}, bf16[16,64,128]{2,1,0:T(8,128)(2,1)S(1)}, u32[]{:S(2)}, u32[]{:S(2)}) collective-permute-start(bf16[16,64,128]{2,1,0:T(8,128)(2,1)S(1)} %get-tuple-element.38), channel_id=1, source_target_pairs={{0,0},{1,2},{2,1},{3,3},{4,64},{5,66},{6,65},{7,67},{8,32},{9,34},... | collective-permute-start | bytes 786440 | tf_op jit(solution)/shard_map/ppermute | solution.py:338
  167.3 1.9 collective-permute-start.15
  171.9 2.5 %shard_map.95 = (bf16[64,64,128]{2,1,0:T(8,128)(2,1)}, f32[8,128]{1,0:T(8,128)S(1)}) custom-call(bf16[16,64,128]{2,1,0:T(8,128)(2,1)S(1)} %collective-permute-done.16.coeffs, bf16[64,64,128]{2,1,0:T(8,128)(2,1)S(1)} %bitcast.45, bf16[64,64,128]{2,1,0:T(8,128)(2,1)S(1)} %bitcast.48, bf16[32,32,128]{2,1,0:T(8,128)(2,1)S(1)} %get-tuple-element.59.refs_0_), custom_call_target="tpu_custom_call" | custom-call | flops 33554432 | bytes 2097152 | tf_op jit(solution)/shard_map/pallas_call | solution.py:359
  175.0 2.5 %shard_map.96 = (bf16[64,64,128]{2,1,0:T(8,128)(2,1)}, f32[8,128]{1,0:T(8,128)S(1)}) custom-call(bf16[16,64,128]{2,1,0:T(8,128)(2,1)S(1)} %collective-permute-done.15.coeffs, bf16[64,64,128]{2,1,0:T(8,128)(2,1)S(1)} %bitcast.46, bf16[64,64,128]{2,1,0:T(8,128)(2,1)S(1)} %bitcast.49, ...), custom_call_target="tpu_custom_call", output_to_operand_aliasing={{0}: (4, {})} | custom-call | flops 33554432 | bytes 2097152 | tf_op jit(solution)/shard_map/pallas_call | solution.py:359
  177.5 20.0 %collective-permute-done.28.received = bf16[32,32,128]{2,1,0:T(8,128)(2,1)S(1)} collective-permute-done((bf16[32,32,128]{2,1,0:T(8,128)(2,1)S(1)}, bf16[32,32,128]{2,1,0:T(8,128)(2,1)S(1)}, u32[]{:S(2)}, u32[]{:S(2)}) %collective-permute-start.28) | collective-permute-done | bytes 262176 | tf_op jit(solution)/shard_map/ppermute | solution.py:328
  199.0 4.1 %collective-permute-done.27.received = bf16[32,32,128]{2,1,0:T(8,128)(2,1)S(1)} collective-permute-done((bf16[32,32,128]{2,1,0:T(8,128)(2,1)S(1)}, bf16[32,32,128]{2,1,0:T(8,128)(2,1)S(1)}, u32[]{:S(2)}, u32[]{:S(2)}) %collective-permute-start.27) | collective-permute-done | bytes 262176 | tf_op jit(solution)/shard_map/ppermute | solution.py:328
  204.4 1.8 shard_map.99.refs_0_
  206.2 1.8 shard_map.100
  (80 shorter events, 33.9 us)
Async XLA Ops:
  0.6 15.7 %copy-start = (bf16[13,64,1,1,64,128]{5,4,3,2,1,0:T(8,128)(2,1)S(1)}, bf16[13,64,1,1,64,128]{5,4,3,2,1,0:T(8,128)(2,1)}, u32[]{:S(2)}) copy-start(bf16[13,64,1,1,64,128]{5,4,3,2,1,0:T(8,128)(2,1)} %param.8) | copy-start | bytes 40894468
  4.5 3.9 %collective-permute-start.1 = (bf16[16,64,128]{2,1,0:T(8,128)(2,1)S(1)}, bf16[16,64,128]{2,1,0:T(8,128)(2,1)S(1)}, u32[]{:S(2)}, u32[]{:S(2)}) collective-permute-start(bf16[16,64,128]{2,1,0:T(8,128)(2,1)S(1)} %shard_map.68.token.own), channel_id=1, source_target_pairs={{0,2},{2,0},{4,6},{6,4},{8,10},{10,8},{12,14},{14,12},{16,18},{18,... | collective-permute-start | bytes 786440 | tf_op jit(solution)/shard_map/ppermute | solution.py:328
  7.0 3.2 %collective-permute-start = (bf16[16,64,128]{2,1,0:T(8,128)(2,1)S(1)}, bf16[16,64,128]{2,1,0:T(8,128)(2,1)S(1)}, u32[]{:S(2)}, u32[]{:S(2)}) collective-permute-start(bf16[16,64,128]{2,1,0:T(8,128)(2,1)S(1)} %shard_map.69.token.own), channel_id=1, source_target_pairs={{0,2},{2,0},{4,6},{6,4},{8,10},{10,8},{12,14},{14,12},{16,18},{18,... | collective-permute-start | bytes 786440 | tf_op jit(solution)/shard_map/ppermute | solution.py:328
  8.9 7.5 %collective-permute-start.3 = (bf16[16,64,128]{2,1,0:T(8,128)(2,1)S(1)}, bf16[16,64,128]{2,1,0:T(8,128)(2,1)S(1)}, u32[]{:S(2)}, u32[]{:S(2)}) collective-permute-start(bf16[16,64,128]{2,1,0:T(8,128)(2,1)S(1)} %shard_map.70.token.own), channel_id=1, source_target_pairs={{0,4},{2,6},{4,0},{6,2},{8,12},{10,14},{12,8},{14,10},{16,20},{18,... | collective-permute-start | bytes 786440 | tf_op jit(solution)/shard_map/ppermute | solution.py:328
  10.7 11.3 %collective-permute-start.2 = (bf16[16,64,128]{2,1,0:T(8,128)(2,1)S(1)}, bf16[16,64,128]{2,1,0:T(8,128)(2,1)S(1)}, u32[]{:S(2)}, u32[]{:S(2)}) collective-permute-start(bf16[16,64,128]{2,1,0:T(8,128)(2,1)S(1)} %shard_map.71.token.own), channel_id=1, source_target_pairs={{0,4},{2,6},{4,0},{6,2},{8,12},{10,14},{12,8},{14,10},{16,20},{18,... | collective-permute-start | bytes 786440 | tf_op jit(solution)/shard_map/ppermute | solution.py:328
  16.8 13.1 %collective-permute-start.5 = (bf16[16,64,128]{2,1,0:T(8,128)(2,1)S(1)}, bf16[16,64,128]{2,1,0:T(8,128)(2,1)S(1)}, u32[]{:S(2)}, u32[]{:S(2)}) collective-permute-start(bf16[16,64,128]{2,1,0:T(8,128)(2,1)S(1)} %shard_map.73.token.own), channel_id=1, source_target_pairs={{0,8},{2,10},{4,12},{6,14},{8,0},{10,2},{12,4},{14,6},{16,24},{18,... | collective-permute-start | bytes 786440 | tf_op jit(solution)/shard_map/ppermute | solution.py:328
  22.4 16.7 %collective-permute-start.4 = (bf16[16,64,128]{2,1,0:T(8,128)(2,1)S(1)}, bf16[16,64,128]{2,1,0:T(8,128)(2,1)S(1)}, u32[]{:S(2)}, u32[]{:S(2)}) collective-permute-start(bf16[16,64,128]{2,1,0:T(8,128)(2,1)S(1)} %shard_map.74.token.own), channel_id=1, source_target_pairs={{0,8},{2,10},{4,12},{6,14},{8,0},{10,2},{12,4},{14,6},{16,24},{18,... | collective-permute-start | bytes 786440 | tf_op jit(solution)/shard_map/ppermute | solution.py:328
  30.3 10.2 %collective-permute-start.7 = (bf16[16,64,128]{2,1,0:T(8,128)(2,1)S(1)}, bf16[16,64,128]{2,1,0:T(8,128)(2,1)S(1)}, u32[]{:S(2)}, u32[]{:S(2)}) collective-permute-start(bf16[16,64,128]{2,1,0:T(8,128)(2,1)S(1)} %shard_map.75.token.own), channel_id=1, source_target_pairs={{0,16},{2,18},{4,20},{6,22},{8,24},{10,26},{12,28},{14,30},{16,0},... | collective-permute-start | bytes 786440 | tf_op jit(solution)/shard_map/ppermute | solution.py:328
  34.0 76.9 %collective-permute-start.13 = (bf16[2,32,64,128]{3,2,1,0:T(8,128)(2,1)S(1)}, bf16[2,32,64,128]{3,2,1,0:T(8,128)(2,1)S(1)}, u32[]{:S(2)}, u32[]{:S(2)}) collective-permute-start(bf16[2,32,64,128]{3,2,1,0:T(8,128)(2,1)S(1)} %shard_map.72.token), channel_id=1, source_target_pairs={{0,0},{1,2},{2,1},{3,3},{4,64},{5,66},{6,65},{7,67},{8,32},{9,34},... | collective-permute-start | bytes 3145736 | tf_op jit(solution)/shard_map/ppermute | solution.py:338
  39.5 18.2 %collective-permute-start.6 = (bf16[16,64,128]{2,1,0:T(8,128)(2,1)S(1)}, bf16[16,64,128]{2,1,0:T(8,128)(2,1)S(1)}, u32[]{:S(2)}, u32[]{:S(2)}) collective-permute-start(bf16[16,64,128]{2,1,0:T(8,128)(2,1)S(1)} %shard_map.76.token.own), channel_id=1, source_target_pairs={{0,16},{2,18},{4,20},{6,22},{8,24},{10,26},{12,28},{14,30},{16,0},... | collective-permute-start | bytes 786440 | tf_op jit(solution)/shard_map/ppermute | solution.py:328
  40.9 52.4 %collective-permute-start.9 = (bf16[16,64,128]{2,1,0:T(8,128)(2,1)S(1)}, bf16[16,64,128]{2,1,0:T(8,128)(2,1)S(1)}, u32[]{:S(2)}, u32[]{:S(2)}) collective-permute-start(bf16[16,64,128]{2,1,0:T(8,128)(2,1)S(1)} %shard_map.77.token.own), channel_id=1, source_target_pairs={{0,32},{2,34},{4,36},{6,38},{8,40},{10,42},{12,44},{14,46},{16,48}... | collective-permute-start | bytes 786440 | tf_op jit(solution)/shard_map/ppermute | solution.py:328
  58.1 40.8 %collective-permute-start.8 = (bf16[16,64,128]{2,1,0:T(8,128)(2,1)S(1)}, bf16[16,64,128]{2,1,0:T(8,128)(2,1)S(1)}, u32[]{:S(2)}, u32[]{:S(2)}) collective-permute-start(bf16[16,64,128]{2,1,0:T(8,128)(2,1)S(1)} %shard_map.78.token.own), channel_id=1, source_target_pairs={{0,32},{2,34},{4,36},{6,38},{8,40},{10,42},{12,44},{14,46},{16,48}... | collective-permute-start | bytes 786440 | tf_op jit(solution)/shard_map/ppermute | solution.py:328
  93.7 10.8 %collective-permute-start.11 = (bf16[16,64,128]{2,1,0:T(8,128)(2,1)S(1)}, bf16[16,64,128]{2,1,0:T(8,128)(2,1)S(1)}, u32[]{:S(2)}, u32[]{:S(2)}) collective-permute-start(bf16[16,64,128]{2,1,0:T(8,128)(2,1)S(1)} %shard_map.79.token.own), channel_id=1, source_target_pairs={{0,64},{2,66},{4,68},{6,70},{8,72},{10,74},{12,76},{14,78},{16,80}... | collective-permute-start | bytes 786440 | tf_op jit(solution)/shard_map/ppermute | solution.py:328
  99.4 10.8 %collective-permute-start.10 = (bf16[16,64,128]{2,1,0:T(8,128)(2,1)S(1)}, bf16[16,64,128]{2,1,0:T(8,128)(2,1)S(1)}, u32[]{:S(2)}, u32[]{:S(2)}) collective-permute-start(bf16[16,64,128]{2,1,0:T(8,128)(2,1)S(1)} %shard_map.80.token.own), channel_id=1, source_target_pairs={{0,64},{2,66},{4,68},{6,70},{8,72},{10,74},{12,76},{14,78},{16,80}... | collective-permute-start | bytes 786440 | tf_op jit(solution)/shard_map/ppermute | solution.py:328
  105.0 7.2 %collective-permute-start.14 = (bf16[16,64,128]{2,1,0:T(8,128)(2,1)S(1)}, bf16[16,64,128]{2,1,0:T(8,128)(2,1)S(1)}, u32[]{:S(2)}, u32[]{:S(2)}) collective-permute-start(bf16[16,64,128]{2,1,0:T(8,128)(2,1)S(1)} %shard_map.81.token.own), channel_id=1, source_target_pairs={{0,1},{1,0},{2,3},{3,2},{4,5},{5,4},{6,7},{7,6},{8,9},{9,8},{10,11... | collective-permute-start | bytes 786440 | tf_op jit(solution)/shard_map/ppermute | solution.py:328
  110.6 7.6 %collective-permute-start.12 = (bf16[16,64,128]{2,1,0:T(8,128)(2,1)S(1)}, bf16[16,64,128]{2,1,0:T(8,128)(2,1)S(1)}, u32[]{:S(2)}, u32[]{:S(2)}) collective-permute-start(bf16[16,64,128]{2,1,0:T(8,128)(2,1)S(1)} %shard_map.82.token.own), channel_id=1, source_target_pairs={{0,1},{1,0},{2,3},{3,2},{4,5},{5,4},{6,7},{7,6},{8,9},{9,8},{10,11... | collective-permute-start | bytes 786440 | tf_op jit(solution)/shard_map/ppermute | solution.py:328
  116.6 6.4 %collective-permute-start.18 = (bf16[32,32,128]{2,1,0:T(8,128)(2,1)S(1)}, bf16[32,32,128]{2,1,0:T(8,128)(2,1)S(1)}, u32[]{:S(2)}, u32[]{:S(2)}) collective-permute-start(bf16[32,32,128]{2,1,0:T(8,128)(2,1)S(1)} %get-tuple-element.36.token), channel_id=1, source_target_pairs={{0,1},{1,0},{2,3},{3,2},{4,5},{5,4},{6,7},{7,6},{8,9},{9,8},{10,11... | collective-permute-start | bytes 786440 | tf_op jit(solution)/shard_map/ppermute | solution.py:328
  122.6 6.5 %collective-permute-start.17 = (bf16[32,32,128]{2,1,0:T(8,128)(2,1)S(1)}, bf16[32,32,128]{2,1,0:T(8,128)(2,1)S(1)}, u32[]{:S(2)}, u32[]{:S(2)}) collective-permute-start(bf16[32,32,128]{2,1,0:T(8,128)(2,1)S(1)} %get-tuple-element.40.token), channel_id=1, source_target_pairs={{0,1},{1,0},{2,3},{3,2},{4,5},{5,4},{6,7},{7,6},{8,9},{9,8},{10,11... | collective-permute-start | bytes 786440 | tf_op jit(solution)/shard_map/ppermute | solution.py:328
  123.5 9.9 %collective-permute-start.20 = (bf16[32,32,128]{2,1,0:T(8,128)(2,1)S(1)}, bf16[32,32,128]{2,1,0:T(8,128)(2,1)S(1)}, u32[]{:S(2)}, u32[]{:S(2)}) collective-permute-start(bf16[32,32,128]{2,1,0:T(8,128)(2,1)S(1)} %get-tuple-element.42.token), channel_id=1, source_target_pairs={{0,64},{2,66},{4,68},{6,70},{8,72},{10,74},{12,76},{14,78},{16,80}... | collective-permute-start | bytes 786440 | tf_op jit(solution)/shard_map/ppermute | solution.py:328
  129.6 8.1 %collective-permute-start.19 = (bf16[32,32,128]{2,1,0:T(8,128)(2,1)S(1)}, bf16[32,32,128]{2,1,0:T(8,128)(2,1)S(1)}, u32[]{:S(2)}, u32[]{:S(2)}) collective-permute-start(bf16[32,32,128]{2,1,0:T(8,128)(2,1)S(1)} %get-tuple-element.44.token), channel_id=1, source_target_pairs={{0,64},{2,66},{4,68},{6,70},{8,72},{10,74},{12,76},{14,78},{16,80}... | collective-permute-start | bytes 786440 | tf_op jit(solution)/shard_map/ppermute | solution.py:328
  133.8 8.4 %collective-permute-start.22 = (bf16[32,32,128]{2,1,0:T(8,128)(2,1)S(1)}, bf16[32,32,128]{2,1,0:T(8,128)(2,1)S(1)}, u32[]{:S(2)}, u32[]{:S(2)}) collective-permute-start(bf16[32,32,128]{2,1,0:T(8,128)(2,1)S(1)} %get-tuple-element.46.token), channel_id=1, source_target_pairs={{0,32},{2,34},{4,36},{6,38},{8,40},{10,42},{12,44},{14,46},{16,48}... | collective-permute-start | bytes 786440 | tf_op jit(solution)/shard_map/ppermute | solution.py:328
  138.1 9.7 %collective-permute-start.21 = (bf16[32,32,128]{2,1,0:T(8,128)(2,1)S(1)}, bf16[32,32,128]{2,1,0:T(8,128)(2,1)S(1)}, u32[]{:S(2)}, u32[]{:S(2)}) collective-permute-start(bf16[32,32,128]{2,1,0:T(8,128)(2,1)S(1)} %get-tuple-element.48.token), channel_id=1, source_target_pairs={{0,32},{2,34},{4,36},{6,38},{8,40},{10,42},{12,44},{14,46},{16,48}... | collective-permute-start | bytes 786440 | tf_op jit(solution)/shard_map/ppermute | solution.py:328
  142.7 6.8 %collective-permute-start.24 = (bf16[32,32,128]{2,1,0:T(8,128)(2,1)S(1)}, bf16[32,32,128]{2,1,0:T(8,128)(2,1)S(1)}, u32[]{:S(2)}, u32[]{:S(2)}) collective-permute-start(bf16[32,32,128]{2,1,0:T(8,128)(2,1)S(1)} %get-tuple-element.50.token), channel_id=1, source_target_pairs={{0,16},{2,18},{4,20},{6,22},{8,24},{10,26},{12,28},{14,30},{16,0},... | collective-permute-start | bytes 786440 | tf_op jit(solution)/shard_map/ppermute | solution.py:328
  148.3 9.0 %collective-permute-start.23 = (bf16[32,32,128]{2,1,0:T(8,128)(2,1)S(1)}, bf16[32,32,128]{2,1,0:T(8,128)(2,1)S(1)}, u32[]{:S(2)}, u32[]{:S(2)}) collective-permute-start(bf16[32,32,128]{2,1,0:T(8,128)(2,1)S(1)} %get-tuple-element.52.token), channel_id=1, source_target_pairs={{0,16},{2,18},{4,20},{6,22},{8,24},{10,26},{12,28},{14,30},{16,0},... | collective-permute-start | bytes 786440 | tf_op jit(solution)/shard_map/ppermute | solution.py:328
  150.0 19.2 %collective-permute-start.26 = (bf16[32,32,128]{2,1,0:T(8,128)(2,1)S(1)}, bf16[32,32,128]{2,1,0:T(8,128)(2,1)S(1)}, u32[]{:S(2)}, u32[]{:S(2)}) collective-permute-start(bf16[32,32,128]{2,1,0:T(8,128)(2,1)S(1)} %get-tuple-element.54.token), channel_id=1, source_target_pairs={{0,8},{2,10},{4,12},{6,14},{8,0},{10,2},{12,4},{14,6},{16,24},{18,... | collective-permute-start | bytes 786440 | tf_op jit(solution)/shard_map/ppermute | solution.py:328
  157.8 13.2 %collective-permute-start.25 = (bf16[32,32,128]{2,1,0:T(8,128)(2,1)S(1)}, bf16[32,32,128]{2,1,0:T(8,128)(2,1)S(1)}, u32[]{:S(2)}, u32[]{:S(2)}) collective-permute-start(bf16[32,32,128]{2,1,0:T(8,128)(2,1)S(1)} %get-tuple-element.56.token), channel_id=1, source_target_pairs={{0,8},{2,10},{4,12},{6,14},{8,0},{10,2},{12,4},{14,6},{16,24},{18,... | collective-permute-start | bytes 786440 | tf_op jit(solution)/shard_map/ppermute | solution.py:328
  160.9 11.0 %collective-permute-start.16 = (bf16[16,64,128]{2,1,0:T(8,128)(2,1)S(1)}, bf16[16,64,128]{2,1,0:T(8,128)(2,1)S(1)}, u32[]{:S(2)}, u32[]{:S(2)}) collective-permute-start(bf16[16,64,128]{2,1,0:T(8,128)(2,1)S(1)} %get-tuple-element.38), channel_id=1, source_target_pairs={{0,0},{1,2},{2,1},{3,3},{4,64},{5,66},{6,65},{7,67},{8,32},{9,34},... | collective-permute-start | bytes 786440 | tf_op jit(solution)/shard_map/ppermute | solution.py:338
  167.3 7.7 %collective-permute-start.15 = (bf16[16,64,128]{2,1,0:T(8,128)(2,1)S(1)}, bf16[16,64,128]{2,1,0:T(8,128)(2,1)S(1)}, u32[]{:S(2)}, u32[]{:S(2)}) collective-permute-start(bf16[16,64,128]{2,1,0:T(8,128)(2,1)S(1)} %get-tuple-element.37), channel_id=1, source_target_pairs={{0,0},{1,2},{2,1},{3,3},{4,64},{5,66},{6,65},{7,67},{8,32},{9,34},... | collective-permute-start | bytes 786440 | tf_op jit(solution)/shard_map/ppermute | solution.py:338
  169.7 27.8 %collective-permute-start.28 = (bf16[32,32,128]{2,1,0:T(8,128)(2,1)S(1)}, bf16[32,32,128]{2,1,0:T(8,128)(2,1)S(1)}, u32[]{:S(2)}, u32[]{:S(2)}) collective-permute-start(bf16[32,32,128]{2,1,0:T(8,128)(2,1)S(1)} %get-tuple-element.58.token), channel_id=1, source_target_pairs={{0,4},{2,6},{4,0},{6,2},{8,12},{10,14},{12,8},{14,10},{16,20},{18,... | collective-permute-start | bytes 786440 | tf_op jit(solution)/shard_map/ppermute | solution.py:328
  171.5 31.6 %collective-permute-start.27 = (bf16[32,32,128]{2,1,0:T(8,128)(2,1)S(1)}, bf16[32,32,128]{2,1,0:T(8,128)(2,1)S(1)}, u32[]{:S(2)}, u32[]{:S(2)}) collective-permute-start(bf16[32,32,128]{2,1,0:T(8,128)(2,1)S(1)} %get-tuple-element.59.refs_0_), channel_id=1, source_target_pairs={{0,4},{2,6},{4,0},{6,2},{8,12},{10,14},{12,8},{14,10},{16,20},{18,... | collective-permute-start | bytes 786440 | tf_op jit(solution)/shard_map/ppermute | solution.py:328
  198.0 6.3 %collective-permute-start.30 = (bf16[32,32,128]{2,1,0:T(8,128)(2,1)S(1)}, bf16[32,32,128]{2,1,0:T(8,128)(2,1)S(1)}, u32[]{:S(2)}, u32[]{:S(2)}) collective-permute-start(bf16[32,32,128]{2,1,0:T(8,128)(2,1)S(1)} %get-tuple-element.66.token), channel_id=1, source_target_pairs={{0,2},{2,0},{4,6},{6,4},{8,10},{10,8},{12,14},{14,12},{16,18},{18,... | collective-permute-start | bytes 786440 | tf_op jit(solution)/shard_map/ppermute | solution.py:328
  203.6 2.5 %collective-permute-start.29 = (bf16[32,32,128]{2,1,0:T(8,128)(2,1)S(1)}, bf16[32,32,128]{2,1,0:T(8,128)(2,1)S(1)}, u32[]{:S(2)}, u32[]{:S(2)}) collective-permute-start(bf16[32,32,128]{2,1,0:T(8,128)(2,1)S(1)} %get-tuple-element.68), channel_id=1, source_target_pairs={{0,2},{2,0},{4,6},{6,4},{8,10},{10,8},{12,14},{14,12},{16,18},{18,... | collective-permute-start | bytes 786440 | tf_op jit(solution)/shard_map/ppermute | solution.py:328
  (7 other events, 17.4 us)
where the time goes:
time: 208 us
  waiting for transfers between devices  120 us (58%)
  starting transfers between devices  47.3 us (23%)
  Pallas kernels  32.8 us (16%)
  local copies, waits for them, and re-layouts  6.59 us (3%)
    ppermute x28, waiting for transfers between devices, exchange(): return lax.ppermute(array, axis, [(i, i ^ 1 << bit) for i in range(count)])  120 us
    ppermute x28, starting transfers between devices, exchange(): return lax.ppermute(array, axis, [(i, i ^ 1 << bit) for i in range(count)])  33.9 us
    ppermute x3, starting transfers between devices, reversal(): return lax.ppermute(array, ('src', 'hi'), pairs_of)  13.4 us
    pallas_call x2, Pallas kernels, body(): middle_call(c)(coeffs[c], exchange(coeffs[c], top), levels, normal, token)  8.8 us
    pallas_call x12, Pallas kernels, body(): adjoint_call(level)(kept[c], exchange(sent[c], level + 1), levels, token)  5.84 us
    unnamed x16, local copies, waits for them, and re-layouts  5.3 us
    pallas_call x12, Pallas kernels, body(): cross_call(level)(coeffs[c], exchange(coeffs[c], level), maps, token)  5.14 us
    pallas_call x2, Pallas kernels, residual_call(): call(kernel, (full_shape, shape(8, LANES, dtype=F32)), specs, (HBM, VMEM)...  4.97 us
  transfers between devices with their start and end apart: 31, of which 19 were waited for; matrix products, arithmetic and copies ran while one was open for 1% of the time, Pallas kernels for 14%

commit v1 on v0

--- a/solution.py
+++ b/solution.py
@@ -47,6 +47,18 @@
     if level < src_bits:
         return (lax.axis_index("src") >> level & 1) == 1
     return (lax.axis_index("hi") >> (level - src_bits) & 1) == 1
+
+
+def shear_x(device):
+    return device ^ reverse_bits(device >> 4 & 3, 2) << 1
+
+
+def shear_y(device):
+    return device ^ reverse_bits(device >> 1 & 3, 2) << 4
+
+
+def swap_ends(device):
+    return device & 62 | device >> 6 | (device & 1) << 6
 
 
 def dot(a, b):
@@ -96,8 +108,8 @@
         out[g] = forward_group(weights, stacked, lane_boxes, rank)
 
 
-def cross_kernel(level, src_bits, lane_boxes, own, other, maps, token, out):
-    cross_step(own, other, maps.at[level], out, is_high(level, src_bits), lane_boxes)
+def cross_kernel(level, src_bits, lane_boxes, own, other, maps, *refs):
+    cross_step(own, other, maps.at[level], refs[-1], is_high(level, src_bits), lane_boxes)
 
 
 def local_forward(lane_boxes, maps, first, out, work):
@@ -129,7 +141,7 @@
                     target[g] = forward_group(weights, stacked, lane_boxes, rank)
 
 
-def prepare_kernel(final_maps, observed, token, out, final, held, sems, wide):
+def prepare_kernel(final_maps, observed, token, gram, right, final, held, sems, wide):
     vectors, boxes, points = held.shape
     rank = final.shape[1]
     box_bits = boxes.bit_length() - 1
@@ -140,7 +152,7 @@
     fetch_maps.wait()
     for p in range(boxes // 2):
         mats = pair_final(final, p, box_bits)
-        out[0, p] = pick_lanes(dot_nt(mats, mats), rank, 2, rank).astype(BF)
+        gram[p] = pick_lanes(dot_nt(mats, mats), rank, 2, rank).astype(BF)
     fetch.wait()
     wide[...] = held[...].astype(F32).reshape(wide.shape)
     for p in range(boxes // 2):
@@ -149,7 +161,7 @@
             for k in (2 * p, 2 * p + 1)
         ]
         product = dot_nt(jnp.concatenate(rows, axis=0).astype(BF), pair_final(final, p, box_bits))
-        out[1, p] = pick_lanes(product, vectors, 2, rank).astype(BF)
+        right[p] = pick_lanes(product, vectors, 2, rank).astype(BF)
 
 
 def pair_final(final, p, box_bits):
@@ -158,30 +170,32 @@
     )
 
 
-def residual_kernel(chunk, coeffs, final_maps, observed, *refs):
-    residual, done, final, held, sems, wide, result = refs[-7:]
-    groups = coeffs.shape[0]
-    vectors, boxes, points = held.shape
+def residual_kernel(chunks, *refs):
+    coeffs = refs[:chunks]
+    final_maps, observed, token, residual, done, final, held, sems, wide = refs[chunks:]
+    groups = coeffs[0].shape[0]
+    total, boxes, points = held.shape
+    vectors = total // chunks
     box_bits = boxes.bit_length() - 1
     lane_boxes = LANES // vectors
-    own_rows = pl.ds(chunk * vectors, vectors)
+    fetch = pltpu.make_async_copy(observed, held, sems.at[0])
+    fetch.start()
     fetch_maps = pltpu.make_async_copy(final_maps, final, sems.at[1])
     fetch_maps.start()
-    fetch = pltpu.make_async_copy(observed.at[own_rows], held, sems.at[0])
-    fetch.start()
     fetch.wait()
     wide[...] = held[...].astype(F32).reshape(wide.shape)
     fetch_maps.wait()
     done[...] = jnp.zeros(done.shape, done.dtype)
     for g in range(groups):
-        turned = jnp.transpose(coeffs[g].astype(F32)).astype(BF)
+        turned = [jnp.transpose(part[g].astype(F32)).astype(BF) for part in coeffs]
         for b in range(lane_boxes):
             t = reverse_bits(g * lane_boxes + b, box_bits)
-            value = dot(turned[b * vectors:(b + 1) * vectors], final[t])
-            rows = pl.ds(t, vectors, stride=boxes)
-            result[rows, :] = value - wide[rows, :]
-    held[...] = result[...].reshape(held.shape).astype(BF)
-    store = pltpu.make_async_copy(held, residual.at[own_rows], sems.at[1])
+            own = [part[b * vectors:(b + 1) * vectors] for part in turned]
+            value = dot(jnp.concatenate(own, axis=0), final[t])
+            rows = pl.ds(t, total, stride=boxes)
+            wide[rows, :] = value - wide[rows, :]
+    held[...] = wide[...].reshape(held.shape).astype(BF)
+    store = pltpu.make_async_copy(held, residual, sems.at[0])
     store.start()
     store.wait()
 
@@ -224,9 +238,9 @@
 
 
 def middle_kernel(
-    level, src_bits, lane_boxes, chunk, own, other, maps, normal, token,
-    coeffs, kept, sent, work, pair_work,
+    level, src_bits, lane_boxes, chunk, own, other, maps, gram, right, *refs,
 ):
+    coeffs, kept, sent, work, pair_work = refs[-5:]
     groups, rank = own.shape[0], own.shape[1]
     pairs, vectors = kept.shape[0], kept.shape[1]
     high = is_high(level, src_bits)
@@ -236,16 +250,17 @@
         turned = jnp.transpose(coeffs[g].astype(F32)).astype(BF)
         for i in range(lane_boxes // 2):
             p = g * lane_boxes // 2 + i
-            product = dot(turned[2 * i * vectors:2 * (i + 1) * vectors], normal[0, p])
+            product = dot(turned[2 * i * vectors:2 * (i + 1) * vectors], gram[p])
             value = pick_lanes(product, vectors, 2, rank)
-            wanted = normal[1, p, pl.ds(chunk * vectors, vectors), :].astype(F32)
+            wanted = right[p, pl.ds(chunk * vectors, vectors), :].astype(F32)
             pair_work[0, p] = (value - wanted).astype(BF)
     source = local_adjoint(maps, level + 1, pair_work)
     for p in range(pairs):
         adjoint_cross_pair(source[p], pair_rows(maps.at[level], p), kept, sent, p, high)
 
 
-def adjoint_cross_kernel(level, src_bits, held_part, received, maps, token, kept, sent):
+def adjoint_cross_kernel(level, src_bits, held_part, received, maps, *refs):
+    kept, sent = refs[-2:]
     high = is_high(level, src_bits)
     for p in range(held_part.shape[0]):
         value = (held_part[p] + received[p].astype(F32)).astype(BF)
@@ -327,15 +342,21 @@
             axis, count, bit = "hi", hi_count, level - src_bits
         return lax.ppermute(array, axis, [(i, i ^ 1 << bit) for i in range(count)])
 
-    def reversal(array):
+    def move(array, after, route):
+        if after is not None:
+            array, _ = lax.optimization_barrier((array, after))
         pairs_of = []
         for src in range(src_count):
             for hi in range(hi_count):
-                there = reverse_bits(hi * src_count + src, device_bits)
+                there = route(hi * src_count + src)
                 pairs_of.append(
                     (src * hi_count + hi, there % src_count * hi_count + there // src_count)
                 )
         return lax.ppermute(array, ("src", "hi"), pairs_of)
+
+    for device in range(src_count * hi_count):
+        along = shear_y(shear_x(swap_ends(shear_y(device))))
+        assert along == reverse_bits(device, device_bits)
 
     def leaf_call(chunk):
         kernel = functools.partial(leaf_kernel, chunk)
@@ -348,17 +369,19 @@
             pltpu.VMEM((total * boxes, points), F32),
         ]
         return call(
-            prepare_kernel, shape(2, pairs, total, LANES), [HBM, HBM, ANY], VMEM, scratch,
+            prepare_kernel, (shape(pairs, rank, LANES), shape(pairs, total, LANES)),
+            [HBM, HBM, ANY], (VMEM, VMEM), scratch,
             4 * flops, 4 * moved, 8,
         )(*operands)
 
-    def residual_call(chunk, *operands):
-        kernel = functools.partial(residual_kernel, chunk)
-        specs = [VMEM, HBM, HBM, ANY] + [HBM] * (len(operands) - 4)
-        scratch = [pltpu.VMEM((boxes, rank, points), BF), held, sems, wide, wide]
+    def residual_call(*operands):
+        scratch = [
+            pltpu.VMEM((boxes, rank, points), BF), pltpu.VMEM((total, boxes, points), BF), sems,
+            pltpu.VMEM((total * boxes, points), F32),
+        ]
         return call(
-            kernel, (full_shape, shape(8, LANES, dtype=F32)), specs, (HBM, VMEM), scratch,
-            flops, 2 * moved, 8, {4: 0} if len(operands) > 4 else None,
+            functools.partial(residual_kernel, CHUNKS), (full_shape, shape(8, LANES, dtype=F32)),
+            [VMEM] * CHUNKS + [HBM, HBM, ANY], (HBM, VMEM), scratch, 2 * flops, 4 * moved, 8,
         )(*operands)
 
     def gradient_call(chunk, *operands):
@@ -369,61 +392,71 @@
             flops, 2 * moved, 8, {3: 0} if len(operands) > 3 else None,
         )(*operands)
 
-    def cross_call(level):
+    def cross_call(level, *operands):
         kernel = functools.partial(cross_kernel, level, src_bits, lane_boxes)
-        return call(kernel, forward_shape, [VMEM] * 3 + [ANY], VMEM, [], flops, moved, 4)
-
-    def adjoint_call(level):
+        specs = [VMEM] * 3 + [ANY] * (len(operands) - 3)
+        return call(kernel, forward_shape, specs, VMEM, [], flops, moved, 4)(*operands)
+
+    def adjoint_call(level, *operands):
         kernel = functools.partial(adjoint_cross_kernel, level, src_bits)
+        specs = [VMEM] * 3 + [ANY] * (len(operands) - 3)
         return call(
-            kernel, (kept_shape, pair_shape), [VMEM] * 3 + [ANY], (VMEM, VMEM), [], flops, moved, 4
-        )
-
-    def middle_call(chunk):
+            kernel, (kept_shape, pair_shape), specs, (VMEM, VMEM), [], flops, moved, 4
+        )(*operands)
+
+    def middle_call(chunk, *operands):
         kernel = functools.partial(middle_kernel, top, src_bits, lane_boxes, chunk)
         scratch = [
             pltpu.VMEM((2, groups, rank, LANES), BF),
             pltpu.VMEM((2, pairs, vectors, LANES), BF),
         ]
+        specs = [VMEM] * 5 + [ANY] * (len(operands) - 5)
         return call(
-            kernel, (forward_shape, kept_shape, pair_shape), [VMEM] * 4 + [ANY], (VMEM,) * 3,
+            kernel, (forward_shape, kept_shape, pair_shape), specs, (VMEM,) * 3,
             scratch, 15 * flops, 15 * moved, 8,
-        )
+        )(*operands)
 
     top = device_bits - 1
+    every, last = range(CHUNKS), CHUNKS - 1
+    coeffs, kept, sent = [None] * CHUNKS, [None] * CHUNKS, [None] * CHUNKS
     token = leaf
-    coeffs, kept, sent, target = [None] * CHUNKS, [None] * CHUNKS, [None] * CHUNKS, [None] * CHUNKS
-    every = range(CHUNKS)
     for c in every:
         coeffs[c] = token = leaf_call(c)(samples, leaf, token)
-    normal = None
     for level in range(top):
+        maps = levels if level else levels[:1]
         for c in every:
-            maps = levels if level else levels[:1]
-            token = cross_call(level)(coeffs[c], exchange(coeffs[c], level), maps, token)
-            coeffs[c] = token
-        if level == 0:
-            normal = token = prepare(final, wanted, token)
-            normal = reversal(normal)
+            operands = (coeffs[c], exchange(coeffs[c], level), maps, token)
+            coeffs[c] = token = cross_call(level, *operands)
+            if (level, c) == (0, last):
+                gram, right = prepare(final, wanted, token)
+                token = right
+            if (level, c) == (0, last):
+                gram, right = (move(x, token, lambda d: swap_ends(shear_y(d))) for x in (gram, right))
+            if (level, c) == (3, 0):
+                gram, right = (move(x, token, shear_x) for x in (gram, right))
+            if (level, c) == (top - 1, 0):
+                gram, right = (move(x, token, shear_y) for x in (gram, right))
+    target = [None] * CHUNKS
     for c in every:
-        target[c], kept[c], sent[c] = middle_call(c)(
-            coeffs[c], exchange(coeffs[c], top), levels, normal, token
-        )
+        operands = (coeffs[c], exchange(coeffs[c], top), levels, gram, right, token)
+        target[c], kept[c], sent[c] = middle_call(c, *operands)
         token = sent[c]
-    residual, gradient = (), ()
+    target = [move(x, None, shear_y) for x in target]
     for level in reversed(range(top)):
         for c in every:
-            kept[c], sent[c] = adjoint_call(level)(
-                kept[c], exchange(sent[c], level + 1), levels, token
-            )
+            operands = (kept[c], exchange(sent[c], level + 1), levels, token)
+            kept[c], sent[c] = adjoint_call(level, *operands)
             token = sent[c]
-        if level == 1:
-            for c in every:
-                operands = (reversal(target[c]), final, wanted, token, *residual)
-                *residual, token = residual_call(c, *operands)
+            if (level, c) == (top - 1, 0):
+                target = [move(x, token, lambda d: swap_ends(shear_x(d))) for x in target]
+            if (level, c) == (top - 3, 0):
+                target = [move(x, token, shear_y) for x in target]
+        if level == top - 4:
+            residual, token = residual_call(*target, final, wanted, token)
+    gradient = ()
     for c in every:
         gradient = [gradient_call(c, kept[c], exchange(sent[c], 0), leaf, *gradient)]
-    residual, gradient = residual[0], gradient[0]
+    gradient = gradient[0]
     return (
         residual.reshape(total, 1, 1, boxes, points),
         gradient.reshape(total, boxes, 1, 1, points),

time: 208 us -> 201 us (0.966)
  waiting for transfers between devices: 120 us -> 48.9 us
  starting transfers between devices: 47.3 us -> 112 us
    ppermute x28, waiting for transfers between devices: 120 us -> 44.4 us  [exchange(): return lax.ppermute(array, axis, [(i, i ^ 1 << bit) for i in range(count)])]
    ppermute x28, starting transfers between devices: 33.9 us -> 89.2 us  [exchange(): return lax.ppermute(array, axis, [(i, i ^ 1 << bit) for i in range(count)])]
    ppermute x3 -> x12, starting transfers between devices: 13.4 us -> 22.7 us  [move(): return lax.ppermute(array, ('src', 'hi'), pairs_of)]
    ppermute x3 -> x12, waiting for transfers between devices: 0.61 us -> 4.48 us  [move(): return lax.ppermute(array, ('src', 'hi'), pairs_of)]
    pallas_call x29 -> x28, Pallas kernels: 27.2 us -> 26.4 us  [the longest x2 8.81 us: middle_call(): call(kernel, (forward_shape, kept_shape, pair_shape), specs, (VMEM,) * 3,...]
  transfers between devices with their start and end apart: 31 -> 40, of which waited for: 19 -> 17; matrix products, arithmetic and copies ran while one was open for 1% -> 1% of each run, Pallas kernels for 14% -> 15%
where the time goes in v1:
time: 201 us
  starting transfers between devices  112 us (56%)
  waiting for transfers between devices  48.9 us (24%)
  Pallas kernels  32 us (16%)
  local copies, waits for them, and re-layouts  6.59 us (3%)
    ppermute x28, starting transfers between devices, exchange(): return lax.ppermute(array, axis, [(i, i ^ 1 << bit) for i in range(count)])  89.2 us
    ppermute x28, waiting for transfers between devices, exchange(): return lax.ppermute(array, axis, [(i, i ^ 1 << bit) for i in range(count)])  44.4 us
    ppermute x12, starting transfers between devices, move(): return lax.ppermute(array, ('src', 'hi'), pairs_of)  22.7 us
    pallas_call x2, Pallas kernels, middle_call(): call(kernel, (forward_shape, kept_shape, pair_shape), specs, (VMEM,) * 3,...  8.81 us
    pallas_call x12, Pallas kernels, adjoint_call(): call(kernel, (kept_shape, pair_shape), specs, (VMEM, VMEM), [], flops, mo...  5.84 us
    unnamed x16, local copies, waits for them, and re-layouts  5.29 us
    pallas_call x12, Pallas kernels, cross_call(): call(kernel, forward_shape, specs, VMEM, [], flops, moved, 4)(*operands)  5.15 us
    ppermute x12, waiting for transfers between devices, move(): return lax.ppermute(array, ('src', 'hi'), pairs_of)  4.48 us
  transfers between devices with their start and end apart: 40, of which 17 were waited for; matrix products, arithmetic and copies ran while one was open for 1% of the time, Pallas kernels for 15%

profile of v1, /device:TPU:1, one launch (start us, length us, event | category | flops | bytes accessed | tf_op | source)
XLA Modules:
  0.0 200.7 jit_solution(1194183318848575689)
XLA Ops:
  13.4 2.4 %shard_map.72 = (bf16[32,64,128]{2,1,0:T(8,128)(2,1)S(1)}, bf16[32,64,128]{2,1,0:T(8,128)(2,1)S(1)}) custom-call(bf16[64,64,128]{2,1,0:T(8,128)(2,1)S(1)} %bitcast.46, bf16[64,64,128]{2,1,0:T(8,128)(2,1)S(1)} %bitcast.48, bf16[16,64,128]{2,1,0:T(8,128)(2,1)S(1)} %shard_map.71.token.own), custom_call_target="tpu_custom_call" | custom-call | flops 134217728 | bytes 4194304 | tf_op jit(solution)/shard_map/pallas_call | solution.py:371
  16.8 2.9 %collective-permute-start.3 = (bf16[16,64,128]{2,1,0:T(8,128)(2,1)S(1)}, bf16[16,64,128]{2,1,0:T(8,128)(2,1)S(1)}, u32[]{:S(2)}, u32[]{:S(2)}) collective-permute-start(bf16[16,64,128]{2,1,0:T(8,128)(2,1)S(1)} %shard_map.73.refs_0_.own), channel_id=1, source_target_pairs={{0,8},{2,10},{4,12},{6,14},{8,0},{10,2},{12,4},{14,6},{16,24},{18,... | collective-permute-start | bytes 786440 | tf_op jit(solution)/shard_map/ppermute | solution.py:343
  19.7 6.0 %collective-permute-start.15 = (bf16[32,64,128]{2,1,0:T(8,128)(2,1)S(1)}, bf16[32,64,128]{2,1,0:T(8,128)(2,1)S(1)}, u32[]{:S(2)}, u32[]{:S(2)}) collective-permute-start(bf16[32,64,128]{2,1,0:T(8,128)(2,1)S(1)} %get-tuple-element.50.refs_0_), channel_id=1, source_target_pairs={{0,0},{1,2},{2,1},{3,3},{4,68},{5,70},{6,69},{7,71},{8,40},{9,42},... | collective-permute-start | bytes 1572872 | tf_op jit(solution)/shard_map/ppermute | solution.py:355
  25.6 1.9 collective-permute-start.12
  30.3 3.7 %collective-permute-start.5 = (bf16[16,64,128]{2,1,0:T(8,128)(2,1)S(1)}, bf16[16,64,128]{2,1,0:T(8,128)(2,1)S(1)}, u32[]{:S(2)}, u32[]{:S(2)}) collective-permute-start(bf16[16,64,128]{2,1,0:T(8,128)(2,1)S(1)} %shard_map.75.refs_0_.own), channel_id=1, source_target_pairs={{0,16},{2,18},{4,20},{6,22},{8,24},{10,26},{12,28},{14,30},{16,0},... | collective-permute-start | bytes 786440 | tf_op jit(solution)/shard_map/ppermute | solution.py:343
  34.0 2.1 %collective-permute-done.6.other = bf16[16,64,128]{2,1,0:T(8,128)(2,1)S(1)} collective-permute-done((bf16[16,64,128]{2,1,0:T(8,128)(2,1)S(1)}, bf16[16,64,128]{2,1,0:T(8,128)(2,1)S(1)}, u32[]{:S(2)}, u32[]{:S(2)}) %collective-permute-start.6) | collective-permute-done | bytes 262176 | tf_op jit(solution)/shard_map/ppermute | solution.py:343
  36.5 3.7 %collective-permute-start.8 = (bf16[16,64,128]{2,1,0:T(8,128)(2,1)S(1)}, bf16[16,64,128]{2,1,0:T(8,128)(2,1)S(1)}, u32[]{:S(2)}, u32[]{:S(2)}) collective-permute-start(bf16[16,64,128]{2,1,0:T(8,128)(2,1)S(1)} %shard_map.76.refs_0_.own), channel_id=1, source_target_pairs={{0,16},{2,18},{4,20},{6,22},{8,24},{10,26},{12,28},{14,30},{16,0},... | collective-permute-start | bytes 786440 | tf_op jit(solution)/shard_map/ppermute | solution.py:343
  40.2 9.3 %collective-permute-done.5.other = bf16[16,64,128]{2,1,0:T(8,128)(2,1)S(1)} collective-permute-done((bf16[16,64,128]{2,1,0:T(8,128)(2,1)S(1)}, bf16[16,64,128]{2,1,0:T(8,128)(2,1)S(1)}, u32[]{:S(2)}, u32[]{:S(2)}) %collective-permute-start.5) | collective-permute-done | bytes 262176 | tf_op jit(solution)/shard_map/ppermute | solution.py:343
  53.2 5.6 %collective-permute-start.10 = (bf16[16,64,128]{2,1,0:T(8,128)(2,1)S(1)}, bf16[16,64,128]{2,1,0:T(8,128)(2,1)S(1)}, u32[]{:S(2)}, u32[]{:S(2)}) collective-permute-start(bf16[16,64,128]{2,1,0:T(8,128)(2,1)S(1)} %shard_map.78.refs_0_.own), channel_id=1, source_target_pairs={{0,32},{2,34},{4,36},{6,38},{8,40},{10,42},{12,44},{14,46},{16,48}... | collective-permute-start | bytes 786440 | tf_op jit(solution)/shard_map/ppermute | solution.py:343
  59.3 2.7 %collective-permute-start.9 = (bf16[16,64,128]{2,1,0:T(8,128)(2,1)S(1)}, bf16[16,64,128]{2,1,0:T(8,128)(2,1)S(1)}, u32[]{:S(2)}, u32[]{:S(2)}) collective-permute-start(bf16[16,64,128]{2,1,0:T(8,128)(2,1)S(1)} %shard_map.79.refs_0_.own), channel_id=1, source_target_pairs={{0,64},{2,66},{4,68},{6,70},{8,72},{10,74},{12,76},{14,78},{16,80}... | collective-permute-start | bytes 786440 | tf_op jit(solution)/shard_map/ppermute | solution.py:343
  64.1 8.8 %collective-permute-done.9.other = bf16[16,64,128]{2,1,0:T(8,128)(2,1)S(1)} collective-permute-done((bf16[16,64,128]{2,1,0:T(8,128)(2,1)S(1)}, bf16[16,64,128]{2,1,0:T(8,128)(2,1)S(1)}, u32[]{:S(2)}, u32[]{:S(2)}) %collective-permute-start.9) | collective-permute-done | bytes 262176 | tf_op jit(solution)/shard_map/ppermute | solution.py:343
  74.7 5.1 %collective-permute-start.18 = (bf16[16,64,128]{2,1,0:T(8,128)(2,1)S(1)}, bf16[16,64,128]{2,1,0:T(8,128)(2,1)S(1)}, u32[]{:S(2)}, u32[]{:S(2)}) collective-permute-start(bf16[16,64,128]{2,1,0:T(8,128)(2,1)S(1)} %shard_map.80.refs_0_.own), channel_id=1, source_target_pairs={{0,64},{2,66},{4,68},{6,70},{8,72},{10,74},{12,76},{14,78},{16,80}... | collective-permute-start | bytes 786440 | tf_op jit(solution)/shard_map/ppermute | solution.py:343
  79.8 6.5 %collective-permute-done.18.other = bf16[16,64,128]{2,1,0:T(8,128)(2,1)S(1)} collective-permute-done((bf16[16,64,128]{2,1,0:T(8,128)(2,1)S(1)}, bf16[16,64,128]{2,1,0:T(8,128)(2,1)S(1)}, u32[]{:S(2)}, u32[]{:S(2)}) %collective-permute-start.18) | collective-permute-done | bytes 262176 | tf_op jit(solution)/shard_map/ppermute | solution.py:343
  87.2 4.4 %shard_map.83 = (bf16[16,64,128]{2,1,0:T(8,128)(2,1)S(1)}, f32[32,32,128]{2,1,0:T(8,128)S(1)}, bf16[32,32,128]{2,1,0:T(8,128)(2,1)S(1)}) custom-call(bf16[16,64,128]{2,1,0:T(8,128)(2,1)S(1)} %shard_map.81.refs_0_.own, bf16[16,64,128]{2,1,0:T(8,128)(2,1)S(1)} %collective-permute-done.11.other, bf16[13,64,64,128]{3,2,1,0:T(8,128)(2,1)S(1)} %bitcast.25, ...), custom_call_target="tpu_custom_call" | custom-call | flops 503316480 | bytes 15728640 | tf_op jit(solution)/shard_map/pallas_call | solution.py:414
  94.0 4.4 %shard_map.84 = (bf16[16,64,128]{2,1,0:T(8,128)(2,1)S(1)}, f32[32,32,128]{2,1,0:T(8,128)S(1)}, bf16[32,32,128]{2,1,0:T(8,128)(2,1)S(1)}) custom-call(bf16[16,64,128]{2,1,0:T(8,128)(2,1)S(1)} %shard_map.82.refs_0_.own, bf16[16,64,128]{2,1,0:T(8,128)(2,1)S(1)} %collective-permute-done.21.other, bf16[13,64,64,128]{3,2,1,0:T(8,128)(2,1)S(1)} %bitcast.26, ...), custom_call_target="tpu_custom_call" | custom-call | flops 503316480 | bytes 15728640 | tf_op jit(solution)/shard_map/pallas_call | solution.py:414
  100.2 2.8 %collective-permute-start.23 = (bf16[32,32,128]{2,1,0:T(8,128)(2,1)S(1)}, bf16[32,32,128]{2,1,0:T(8,128)(2,1)S(1)}, u32[]{:S(2)}, u32[]{:S(2)}) collective-permute-start(bf16[32,32,128]{2,1,0:T(8,128)(2,1)S(1)} %get-tuple-element.57.refs_0_), channel_id=1, source_target_pairs={{0,64},{2,66},{4,68},{6,70},{8,72},{10,74},{12,76},{14,78},{16,80}... | collective-permute-start | bytes 786440 | tf_op jit(solution)/shard_map/ppermute | solution.py:343
  104.2 2.4 %collective-permute-start.26 = (bf16[32,32,128]{2,1,0:T(8,128)(2,1)S(1)}, bf16[32,32,128]{2,1,0:T(8,128)(2,1)S(1)}, u32[]{:S(2)}, u32[]{:S(2)}) collective-permute-start(bf16[32,32,128]{2,1,0:T(8,128)(2,1)S(1)} %get-tuple-element.61.refs_0_), channel_id=1, source_target_pairs={{0,64},{2,66},{4,68},{6,70},{8,72},{10,74},{12,76},{14,78},{16,80}... | collective-permute-start | bytes 786440 | tf_op jit(solution)/shard_map/ppermute | solution.py:343
  108.7 2.8 %collective-permute-start.25 = (bf16[32,32,128]{2,1,0:T(8,128)(2,1)S(1)}, bf16[32,32,128]{2,1,0:T(8,128)(2,1)S(1)}, u32[]{:S(2)}, u32[]{:S(2)}) collective-permute-start(bf16[32,32,128]{2,1,0:T(8,128)(2,1)S(1)} %get-tuple-element.63.refs_0_), channel_id=1, source_target_pairs={{0,32},{2,34},{4,36},{6,38},{8,40},{10,42},{12,44},{14,46},{16,48}... | collective-permute-start | bytes 786440 | tf_op jit(solution)/shard_map/ppermute | solution.py:343
  111.5 1.9 collective-permute-done.26.received
  113.9 1.9 collective-permute-start.31
  115.8 7.4 %collective-permute-start.29 = (bf16[16,64,128]{2,1,0:T(8,128)(2,1)S(1)}, bf16[16,64,128]{2,1,0:T(8,128)(2,1)S(1)}, u32[]{:S(2)}, u32[]{:S(2)}) collective-permute-start(bf16[16,64,128]{2,1,0:T(8,128)(2,1)S(1)} %collective-permute-done.28), channel_id=1, source_target_pairs={{0,0},{1,2},{2,1},{3,3},{4,4},{5,6},{6,5},{7,7},{8,8},{9,10},{10,9... | collective-permute-start | bytes 786440 | tf_op jit(solution)/shard_map/ppermute | solution.py:355
  123.2 1.9 collective-permute-start.22
  127.1 2.2 %collective-permute-start.32 = (bf16[32,32,128]{2,1,0:T(8,128)(2,1)S(1)}, bf16[32,32,128]{2,1,0:T(8,128)(2,1)S(1)}, u32[]{:S(2)}, u32[]{:S(2)}) collective-permute-start(bf16[32,32,128]{2,1,0:T(8,128)(2,1)S(1)} %get-tuple-element.73.refs_0_), channel_id=1, source_target_pairs={{0,16},{2,18},{4,20},{6,22},{8,24},{10,26},{12,28},{14,30},{16,0},... | collective-permute-start | bytes 786440 | tf_op jit(solution)/shard_map/ppermute | solution.py:343
  129.3 4.4 %collective-permute-done.22 = bf16[16,64,128]{2,1,0:T(8,128)(2,1)S(1)} collective-permute-done((bf16[16,64,128]{2,1,0:T(8,128)(2,1)S(1)}, bf16[16,64,128]{2,1,0:T(8,128)(2,1)S(1)}, u32[]{:S(2)}, u32[]{:S(2)}) %collective-permute-start.22) | collective-permute-done | bytes 262176 | tf_op jit(solution)/shard_map/ppermute | solution.py:355
  135.1 2.1 %collective-permute-done.33.received = bf16[32,32,128]{2,1,0:T(8,128)(2,1)S(1)} collective-permute-done((bf16[32,32,128]{2,1,0:T(8,128)(2,1)S(1)}, bf16[32,32,128]{2,1,0:T(8,128)(2,1)S(1)}, u32[]{:S(2)}, u32[]{:S(2)}) %collective-permute-start.33) | collective-permute-done | bytes 262176 | tf_op jit(solution)/shard_map/ppermute | solution.py:343
  137.7 28.2 %collective-permute-start.35 = (bf16[32,32,128]{2,1,0:T(8,128)(2,1)S(1)}, bf16[32,32,128]{2,1,0:T(8,128)(2,1)S(1)}, u32[]{:S(2)}, u32[]{:S(2)}) collective-permute-start(bf16[32,32,128]{2,1,0:T(8,128)(2,1)S(1)} %get-tuple-element.75.refs_0_), channel_id=1, source_target_pairs={{0,8},{2,10},{4,12},{6,14},{8,0},{10,2},{12,4},{14,6},{16,24},{18,... | collective-permute-start | bytes 786440 | tf_op jit(solution)/shard_map/ppermute | solution.py:343
  166.4 2.7 %collective-permute-start.34 = (bf16[32,32,128]{2,1,0:T(8,128)(2,1)S(1)}, bf16[32,32,128]{2,1,0:T(8,128)(2,1)S(1)}, u32[]{:S(2)}, u32[]{:S(2)}) collective-permute-start(bf16[32,32,128]{2,1,0:T(8,128)(2,1)S(1)} %get-tuple-element.76.refs_4_), channel_id=1, source_target_pairs={{0,8},{2,10},{4,12},{6,14},{8,0},{10,2},{12,4},{14,6},{16,24},{18,... | collective-permute-start | bytes 786440 | tf_op jit(solution)/shard_map/ppermute | solution.py:343
  169.1 4.1 %shard_map.93 = (bf16[64,64,128]{2,1,0:T(8,128)(2,1)}, f32[8,128]{1,0:T(8,128)S(1)}) custom-call(bf16[16,64,128]{2,1,0:T(8,128)(2,1)S(1)} %collective-permute-done.27.refs_0_, bf16[16,64,128]{2,1,0:T(8,128)(2,1)S(1)} %collective-permute-done.30.refs_1_, bf16[64,64,128]{2,1,0:T(8,128)(2,1)S(1)} %bitcast.47, bf16[64,64,128]{2,1,0:T(8,128)(2,1)S(1)} %bitcast.49, ...), custom_call_target="tpu_custom_call" | custom-call | flops 67108864 | bytes 4194304 | tf_op jit(solution)/shard_map/pallas_call | solution.py:382
  173.8 9.7 %collective-permute-start.37 = (bf16[32,32,128]{2,1,0:T(8,128)(2,1)S(1)}, bf16[32,32,128]{2,1,0:T(8,128)(2,1)S(1)}, u32[]{:S(2)}, u32[]{:S(2)}) collective-permute-start(bf16[32,32,128]{2,1,0:T(8,128)(2,1)S(1)} %get-tuple-element.81.refs_0_), channel_id=1, source_target_pairs={{0,4},{2,6},{4,0},{6,2},{8,12},{10,14},{12,8},{14,10},{16,20},{18,... | collective-permute-start | bytes 786440 | tf_op jit(solution)/shard_map/ppermute | solution.py:343
  184.2 5.1 %collective-permute-done.37.received = bf16[32,32,128]{2,1,0:T(8,128)(2,1)S(1)} collective-permute-done((bf16[32,32,128]{2,1,0:T(8,128)(2,1)S(1)}, bf16[32,32,128]{2,1,0:T(8,128)(2,1)S(1)}, u32[]{:S(2)}, u32[]{:S(2)}) %collective-permute-start.37) | collective-permute-done | bytes 262176 | tf_op jit(solution)/shard_map/ppermute | solution.py:343
  189.8 2.5 %collective-permute-start.39 = (bf16[32,32,128]{2,1,0:T(8,128)(2,1)S(1)}, bf16[32,32,128]{2,1,0:T(8,128)(2,1)S(1)}, u32[]{:S(2)}, u32[]{:S(2)}) collective-permute-start(bf16[32,32,128]{2,1,0:T(8,128)(2,1)S(1)} %get-tuple-element.85.refs_0_), channel_id=1, source_target_pairs={{0,2},{2,0},{4,6},{6,4},{8,10},{10,8},{12,14},{14,12},{16,18},{18,... | collective-permute-start | bytes 786440 | tf_op jit(solution)/shard_map/ppermute | solution.py:343
  192.3 2.6 %collective-permute-done.36.received = bf16[32,32,128]{2,1,0:T(8,128)(2,1)S(1)} collective-permute-done((bf16[32,32,128]{2,1,0:T(8,128)(2,1)S(1)}, bf16[32,32,128]{2,1,0:T(8,128)(2,1)S(1)}, u32[]{:S(2)}, u32[]{:S(2)}) %collective-permute-start.36) | collective-permute-done | bytes 262176 | tf_op jit(solution)/shard_map/ppermute | solution.py:343
  (97 shorter events, 45.0 us)
Async XLA Ops:
  10.7 16.9 %collective-permute-start.4 = (bf16[16,64,128]{2,1,0:T(8,128)(2,1)S(1)}, bf16[16,64,128]{2,1,0:T(8,128)(2,1)S(1)}, u32[]{:S(2)}, u32[]{:S(2)}) collective-permute-start(bf16[16,64,128]{2,1,0:T(8,128)(2,1)S(1)} %shard_map.71.token.own), channel_id=1, source_target_pairs={{0,4},{2,6},{4,0},{6,2},{8,12},{10,14},{12,8},{14,10},{16,20},{18,... | collective-permute-start | bytes 786440 | tf_op jit(solution)/shard_map/ppermute | solution.py:343
  16.8 13.1 %collective-permute-start.3 = (bf16[16,64,128]{2,1,0:T(8,128)(2,1)S(1)}, bf16[16,64,128]{2,1,0:T(8,128)(2,1)S(1)}, u32[]{:S(2)}, u32[]{:S(2)}) collective-permute-start(bf16[16,64,128]{2,1,0:T(8,128)(2,1)S(1)} %shard_map.73.refs_0_.own), channel_id=1, source_target_pairs={{0,8},{2,10},{4,12},{6,14},{8,0},{10,2},{12,4},{14,6},{16,24},{18,... | collective-permute-start | bytes 786440 | tf_op jit(solution)/shard_map/ppermute | solution.py:343
  19.7 31.7 %collective-permute-start.15 = (bf16[32,64,128]{2,1,0:T(8,128)(2,1)S(1)}, bf16[32,64,128]{2,1,0:T(8,128)(2,1)S(1)}, u32[]{:S(2)}, u32[]{:S(2)}) collective-permute-start(bf16[32,64,128]{2,1,0:T(8,128)(2,1)S(1)} %get-tuple-element.50.refs_0_), channel_id=1, source_target_pairs={{0,0},{1,2},{2,1},{3,3},{4,68},{5,70},{6,69},{7,71},{8,40},{9,42},... | collective-permute-start | bytes 1572872 | tf_op jit(solution)/shard_map/ppermute | solution.py:355
  25.6 26.4 %collective-permute-start.12 = (bf16[32,64,128]{2,1,0:T(8,128)(2,1)S(1)}, bf16[32,64,128]{2,1,0:T(8,128)(2,1)S(1)}, u32[]{:S(2)}, u32[]{:S(2)}) collective-permute-start(bf16[32,64,128]{2,1,0:T(8,128)(2,1)S(1)} %get-tuple-element.47), channel_id=1, source_target_pairs={{0,0},{1,2},{2,1},{3,3},{4,68},{5,70},{6,69},{7,71},{8,40},{9,42},... | collective-permute-start | bytes 1572872 | tf_op jit(solution)/shard_map/ppermute | solution.py:355
  28.0 8.1 %collective-permute-start.6 = (bf16[16,64,128]{2,1,0:T(8,128)(2,1)S(1)}, bf16[16,64,128]{2,1,0:T(8,128)(2,1)S(1)}, u32[]{:S(2)}, u32[]{:S(2)}) collective-permute-start(bf16[16,64,128]{2,1,0:T(8,128)(2,1)S(1)} %shard_map.74.refs_0_.own), channel_id=1, source_target_pairs={{0,8},{2,10},{4,12},{6,14},{8,0},{10,2},{12,4},{14,6},{16,24},{18,... | collective-permute-start | bytes 786440 | tf_op jit(solution)/shard_map/ppermute | solution.py:343
  30.3 19.3 %collective-permute-start.5 = (bf16[16,64,128]{2,1,0:T(8,128)(2,1)S(1)}, bf16[16,64,128]{2,1,0:T(8,128)(2,1)S(1)}, u32[]{:S(2)}, u32[]{:S(2)}) collective-permute-start(bf16[16,64,128]{2,1,0:T(8,128)(2,1)S(1)} %shard_map.75.refs_0_.own), channel_id=1, source_target_pairs={{0,16},{2,18},{4,20},{6,22},{8,24},{10,26},{12,28},{14,30},{16,0},... | collective-permute-start | bytes 786440 | tf_op jit(solution)/shard_map/ppermute | solution.py:343
  36.5 16.2 %collective-permute-start.8 = (bf16[16,64,128]{2,1,0:T(8,128)(2,1)S(1)}, bf16[16,64,128]{2,1,0:T(8,128)(2,1)S(1)}, u32[]{:S(2)}, u32[]{:S(2)}) collective-permute-start(bf16[16,64,128]{2,1,0:T(8,128)(2,1)S(1)} %shard_map.76.refs_0_.own), channel_id=1, source_target_pairs={{0,16},{2,18},{4,20},{6,22},{8,24},{10,26},{12,28},{14,30},{16,0},... | collective-permute-start | bytes 786440 | tf_op jit(solution)/shard_map/ppermute | solution.py:343
  50.0 8.9 %collective-permute-start.7 = (bf16[16,64,128]{2,1,0:T(8,128)(2,1)S(1)}, bf16[16,64,128]{2,1,0:T(8,128)(2,1)S(1)}, u32[]{:S(2)}, u32[]{:S(2)}) collective-permute-start(bf16[16,64,128]{2,1,0:T(8,128)(2,1)S(1)} %shard_map.77.refs_0_.own), channel_id=1, source_target_pairs={{0,32},{2,34},{4,36},{6,38},{8,40},{10,42},{12,44},{14,46},{16,48}... | collective-permute-start | bytes 786440 | tf_op jit(solution)/shard_map/ppermute | solution.py:343
  51.4 21.9 %collective-permute-start.16 = (bf16[32,64,128]{2,1,0:T(8,128)(2,1)S(1)}, bf16[32,64,128]{2,1,0:T(8,128)(2,1)S(1)}, u32[]{:S(2)}, u32[]{:S(2)}) collective-permute-start(bf16[32,64,128]{2,1,0:T(8,128)(2,1)S(1)} %collective-permute-done.15), channel_id=1, source_target_pairs={{0,0},{1,1},{2,2},{3,3},{4,4},{5,5},{6,6},{7,7},{8,8},{9,9},{10,10... | collective-permute-start | bytes 1572872 | tf_op jit(solution)/shard_map/ppermute | solution.py:355
  52.1 22.0 %collective-permute-start.13 = (bf16[32,64,128]{2,1,0:T(8,128)(2,1)S(1)}, bf16[32,64,128]{2,1,0:T(8,128)(2,1)S(1)}, u32[]{:S(2)}, u32[]{:S(2)}) collective-permute-start(bf16[32,64,128]{2,1,0:T(8,128)(2,1)S(1)} %collective-permute-done.12), channel_id=1, source_target_pairs={{0,0},{1,1},{2,2},{3,3},{4,4},{5,5},{6,6},{7,7},{8,8},{9,9},{10,10... | collective-permute-start | bytes 1572872 | tf_op jit(solution)/shard_map/ppermute | solution.py:355
  53.2 10.4 %collective-permute-start.10 = (bf16[16,64,128]{2,1,0:T(8,128)(2,1)S(1)}, bf16[16,64,128]{2,1,0:T(8,128)(2,1)S(1)}, u32[]{:S(2)}, u32[]{:S(2)}) collective-permute-start(bf16[16,64,128]{2,1,0:T(8,128)(2,1)S(1)} %shard_map.78.refs_0_.own), channel_id=1, source_target_pairs={{0,32},{2,34},{4,36},{6,38},{8,40},{10,42},{12,44},{14,46},{16,48}... | collective-permute-start | bytes 786440 | tf_op jit(solution)/shard_map/ppermute | solution.py:343
  59.3 13.6 %collective-permute-start.9 = (bf16[16,64,128]{2,1,0:T(8,128)(2,1)S(1)}, bf16[16,64,128]{2,1,0:T(8,128)(2,1)S(1)}, u32[]{:S(2)}, u32[]{:S(2)}) collective-permute-start(bf16[16,64,128]{2,1,0:T(8,128)(2,1)S(1)} %shard_map.79.refs_0_.own), channel_id=1, source_target_pairs={{0,64},{2,66},{4,68},{6,70},{8,72},{10,74},{12,76},{14,78},{16,80}... | collective-permute-start | bytes 786440 | tf_op jit(solution)/shard_map/ppermute | solution.py:343
  73.3 13.9 %collective-permute-start.17 = (bf16[32,64,128]{2,1,0:T(8,128)(2,1)S(1)}, bf16[32,64,128]{2,1,0:T(8,128)(2,1)S(1)}, u32[]{:S(2)}, u32[]{:S(2)}) collective-permute-start(bf16[32,64,128]{2,1,0:T(8,128)(2,1)S(1)} %collective-permute-done.16), channel_id=1, source_target_pairs={{0,0},{1,1},{2,2},{3,3},{4,68},{5,69},{6,70},{7,71},{8,40},{9,41},... | collective-permute-start | bytes 1572872 | tf_op jit(solution)/shard_map/ppermute | solution.py:355
  74.0 13.2 %collective-permute-start.14 = (bf16[32,64,128]{2,1,0:T(8,128)(2,1)S(1)}, bf16[32,64,128]{2,1,0:T(8,128)(2,1)S(1)}, u32[]{:S(2)}, u32[]{:S(2)}) collective-permute-start(bf16[32,64,128]{2,1,0:T(8,128)(2,1)S(1)} %collective-permute-done.13), channel_id=1, source_target_pairs={{0,0},{1,1},{2,2},{3,3},{4,68},{5,69},{6,70},{7,71},{8,40},{9,41},... | collective-permute-start | bytes 1572872 | tf_op jit(solution)/shard_map/ppermute | solution.py:355
  74.7 11.6 %collective-permute-start.18 = (bf16[16,64,128]{2,1,0:T(8,128)(2,1)S(1)}, bf16[16,64,128]{2,1,0:T(8,128)(2,1)S(1)}, u32[]{:S(2)}, u32[]{:S(2)}) collective-permute-start(bf16[16,64,128]{2,1,0:T(8,128)(2,1)S(1)} %shard_map.80.refs_0_.own), channel_id=1, source_target_pairs={{0,64},{2,66},{4,68},{6,70},{8,72},{10,74},{12,76},{14,78},{16,80}... | collective-permute-start | bytes 786440 | tf_op jit(solution)/shard_map/ppermute | solution.py:343
  91.6 8.2 %collective-permute-start.20 = (bf16[32,32,128]{2,1,0:T(8,128)(2,1)S(1)}, bf16[32,32,128]{2,1,0:T(8,128)(2,1)S(1)}, u32[]{:S(2)}, u32[]{:S(2)}) collective-permute-start(bf16[32,32,128]{2,1,0:T(8,128)(2,1)S(1)} %get-tuple-element.55.refs_0_), channel_id=1, source_target_pairs={{0,1},{1,0},{2,3},{3,2},{4,5},{5,4},{6,7},{7,6},{8,9},{9,8},{10,11... | collective-permute-start | bytes 786440 | tf_op jit(solution)/shard_map/ppermute | solution.py:343
  100.2 7.9 %collective-permute-start.23 = (bf16[32,32,128]{2,1,0:T(8,128)(2,1)S(1)}, bf16[32,32,128]{2,1,0:T(8,128)(2,1)S(1)}, u32[]{:S(2)}, u32[]{:S(2)}) collective-permute-start(bf16[32,32,128]{2,1,0:T(8,128)(2,1)S(1)} %get-tuple-element.57.refs_0_), channel_id=1, source_target_pairs={{0,64},{2,66},{4,68},{6,70},{8,72},{10,74},{12,76},{14,78},{16,80}... | collective-permute-start | bytes 786440 | tf_op jit(solution)/shard_map/ppermute | solution.py:343
  104.2 9.2 %collective-permute-start.26 = (bf16[32,32,128]{2,1,0:T(8,128)(2,1)S(1)}, bf16[32,32,128]{2,1,0:T(8,128)(2,1)S(1)}, u32[]{:S(2)}, u32[]{:S(2)}) collective-permute-start(bf16[32,32,128]{2,1,0:T(8,128)(2,1)S(1)} %get-tuple-element.61.refs_0_), channel_id=1, source_target_pairs={{0,64},{2,66},{4,68},{6,70},{8,72},{10,74},{12,76},{14,78},{16,80}... | collective-permute-start | bytes 786440 | tf_op jit(solution)/shard_map/ppermute | solution.py:343
  106.6 16.6 %collective-permute-start.19 = (bf16[16,64,128]{2,1,0:T(8,128)(2,1)S(1)}, bf16[16,64,128]{2,1,0:T(8,128)(2,1)S(1)}, u32[]{:S(2)}, u32[]{:S(2)}) collective-permute-start(bf16[16,64,128]{2,1,0:T(8,128)(2,1)S(1)} %get-tuple-element.53), channel_id=1, source_target_pairs={{0,0},{1,1},{2,2},{3,3},{4,68},{5,69},{6,70},{7,71},{8,40},{9,41},... | collective-permute-start | bytes 786440 | tf_op jit(solution)/shard_map/ppermute | solution.py:355
  107.2 8.5 %collective-permute-start.28 = (bf16[16,64,128]{2,1,0:T(8,128)(2,1)S(1)}, bf16[16,64,128]{2,1,0:T(8,128)(2,1)S(1)}, u32[]{:S(2)}, u32[]{:S(2)}) collective-permute-start(bf16[16,64,128]{2,1,0:T(8,128)(2,1)S(1)} %get-tuple-element.68), channel_id=1, source_target_pairs={{0,0},{1,1},{2,2},{3,3},{4,68},{5,69},{6,70},{7,71},{8,40},{9,41},... | collective-permute-start | bytes 786440 | tf_op jit(solution)/shard_map/ppermute | solution.py:355
  108.7 16.5 %collective-permute-start.25 = (bf16[32,32,128]{2,1,0:T(8,128)(2,1)S(1)}, bf16[32,32,128]{2,1,0:T(8,128)(2,1)S(1)}, u32[]{:S(2)}, u32[]{:S(2)}) collective-permute-start(bf16[32,32,128]{2,1,0:T(8,128)(2,1)S(1)} %get-tuple-element.63.refs_0_), channel_id=1, source_target_pairs={{0,32},{2,34},{4,36},{6,38},{8,40},{10,42},{12,44},{14,46},{16,48}... | collective-permute-start | bytes 786440 | tf_op jit(solution)/shard_map/ppermute | solution.py:343
  113.9 12.7 %collective-permute-start.31 = (bf16[32,32,128]{2,1,0:T(8,128)(2,1)S(1)}, bf16[32,32,128]{2,1,0:T(8,128)(2,1)S(1)}, u32[]{:S(2)}, u32[]{:S(2)}) collective-permute-start(bf16[32,32,128]{2,1,0:T(8,128)(2,1)S(1)} %get-tuple-element.65.refs_0_), channel_id=1, source_target_pairs={{0,32},{2,34},{4,36},{6,38},{8,40},{10,42},{12,44},{14,46},{16,48}... | collective-permute-start | bytes 786440 | tf_op jit(solution)/shard_map/ppermute | solution.py:343
  115.8 13.5 %collective-permute-start.29 = (bf16[16,64,128]{2,1,0:T(8,128)(2,1)S(1)}, bf16[16,64,128]{2,1,0:T(8,128)(2,1)S(1)}, u32[]{:S(2)}, u32[]{:S(2)}) collective-permute-start(bf16[16,64,128]{2,1,0:T(8,128)(2,1)S(1)} %collective-permute-done.28), channel_id=1, source_target_pairs={{0,0},{1,2},{2,1},{3,3},{4,4},{5,6},{6,5},{7,7},{8,8},{9,10},{10,9... | collective-permute-start | bytes 786440 | tf_op jit(solution)/shard_map/ppermute | solution.py:355
  123.2 10.5 %collective-permute-start.22 = (bf16[16,64,128]{2,1,0:T(8,128)(2,1)S(1)}, bf16[16,64,128]{2,1,0:T(8,128)(2,1)S(1)}, u32[]{:S(2)}, u32[]{:S(2)}) collective-permute-start(bf16[16,64,128]{2,1,0:T(8,128)(2,1)S(1)} %collective-permute-done.19), channel_id=1, source_target_pairs={{0,0},{1,2},{2,1},{3,3},{4,4},{5,6},{6,5},{7,7},{8,8},{9,10},{10,9... | collective-permute-start | bytes 786440 | tf_op jit(solution)/shard_map/ppermute | solution.py:355
  125.7 11.5 %collective-permute-start.33 = (bf16[32,32,128]{2,1,0:T(8,128)(2,1)S(1)}, bf16[32,32,128]{2,1,0:T(8,128)(2,1)S(1)}, u32[]{:S(2)}, u32[]{:S(2)}) collective-permute-start(bf16[32,32,128]{2,1,0:T(8,128)(2,1)S(1)} %get-tuple-element.66.refs_0_), channel_id=1, source_target_pairs={{0,16},{2,18},{4,20},{6,22},{8,24},{10,26},{12,28},{14,30},{16,0},... | collective-permute-start | bytes 786440 | tf_op jit(solution)/shard_map/ppermute | solution.py:343
  127.1 38.8 %collective-permute-start.32 = (bf16[32,32,128]{2,1,0:T(8,128)(2,1)S(1)}, bf16[32,32,128]{2,1,0:T(8,128)(2,1)S(1)}, u32[]{:S(2)}, u32[]{:S(2)}) collective-permute-start(bf16[32,32,128]{2,1,0:T(8,128)(2,1)S(1)} %get-tuple-element.73.refs_0_), channel_id=1, source_target_pairs={{0,16},{2,18},{4,20},{6,22},{8,24},{10,26},{12,28},{14,30},{16,0},... | collective-permute-start | bytes 786440 | tf_op jit(solution)/shard_map/ppermute | solution.py:343
  133.7 35.4 %collective-permute-start.27 = (bf16[16,64,128]{2,1,0:T(8,128)(2,1)S(1)}, bf16[16,64,128]{2,1,0:T(8,128)(2,1)S(1)}, u32[]{:S(2)}, u32[]{:S(2)}) collective-permute-start(bf16[16,64,128]{2,1,0:T(8,128)(2,1)S(1)} %collective-permute-done.22), channel_id=1, source_target_pairs={{0,0},{1,1},{2,2},{3,3},{4,68},{5,69},{6,70},{7,71},{8,40},{9,41},... | collective-permute-start | bytes 786440 | tf_op jit(solution)/shard_map/ppermute | solution.py:355
  134.4 34.7 %collective-permute-start.30 = (bf16[16,64,128]{2,1,0:T(8,128)(2,1)S(1)}, bf16[16,64,128]{2,1,0:T(8,128)(2,1)S(1)}, u32[]{:S(2)}, u32[]{:S(2)}) collective-permute-start(bf16[16,64,128]{2,1,0:T(8,128)(2,1)S(1)} %collective-permute-done.29), channel_id=1, source_target_pairs={{0,0},{1,1},{2,2},{3,3},{4,68},{5,69},{6,70},{7,71},{8,40},{9,41},... | collective-permute-start | bytes 786440 | tf_op jit(solution)/shard_map/ppermute | solution.py:355
  137.7 35.6 %collective-permute-start.35 = (bf16[32,32,128]{2,1,0:T(8,128)(2,1)S(1)}, bf16[32,32,128]{2,1,0:T(8,128)(2,1)S(1)}, u32[]{:S(2)}, u32[]{:S(2)}) collective-permute-start(bf16[32,32,128]{2,1,0:T(8,128)(2,1)S(1)} %get-tuple-element.75.refs_0_), channel_id=1, source_target_pairs={{0,8},{2,10},{4,12},{6,14},{8,0},{10,2},{12,4},{14,6},{16,24},{18,... | collective-permute-start | bytes 786440 | tf_op jit(solution)/shard_map/ppermute | solution.py:343
  166.4 17.0 %collective-permute-start.34 = (bf16[32,32,128]{2,1,0:T(8,128)(2,1)S(1)}, bf16[32,32,128]{2,1,0:T(8,128)(2,1)S(1)}, u32[]{:S(2)}, u32[]{:S(2)}) collective-permute-start(bf16[32,32,128]{2,1,0:T(8,128)(2,1)S(1)} %get-tuple-element.76.refs_4_), channel_id=1, source_target_pairs={{0,8},{2,10},{4,12},{6,14},{8,0},{10,2},{12,4},{14,6},{16,24},{18,... | collective-permute-start | bytes 786440 | tf_op jit(solution)/shard_map/ppermute | solution.py:343
  173.8 15.5 %collective-permute-start.37 = (bf16[32,32,128]{2,1,0:T(8,128)(2,1)S(1)}, bf16[32,32,128]{2,1,0:T(8,128)(2,1)S(1)}, u32[]{:S(2)}, u32[]{:S(2)}) collective-permute-start(bf16[32,32,128]{2,1,0:T(8,128)(2,1)S(1)} %get-tuple-element.81.refs_0_), channel_id=1, source_target_pairs={{0,4},{2,6},{4,0},{6,2},{8,12},{10,14},{12,8},{14,10},{16,20},{18,... | collective-permute-start | bytes 786440 | tf_op jit(solution)/shard_map/ppermute | solution.py:343
  183.9 11.0 %collective-permute-start.36 = (bf16[32,32,128]{2,1,0:T(8,128)(2,1)S(1)}, bf16[32,32,128]{2,1,0:T(8,128)(2,1)S(1)}, u32[]{:S(2)}, u32[]{:S(2)}) collective-permute-start(bf16[32,32,128]{2,1,0:T(8,128)(2,1)S(1)} %get-tuple-element.83.refs_0_), channel_id=1, source_target_pairs={{0,4},{2,6},{4,0},{6,2},{8,12},{10,14},{12,8},{14,10},{16,20},{18,... | collective-permute-start | bytes 786440 | tf_op jit(solution)/shard_map/ppermute | solution.py:343
  (16 other events, 137.3 us)
